TPU v7x, 512 devices: a whole 4x8x8 slice. The times are simulated.
512 devices in a mesh: dp: 64 (over y_lo, x, z), tensor: 8 (over y_hi, core).
Axes of the slice: x: 4, y: 8 (y_hi: 4, y_lo: 2; y = y_hi * 2 + y_lo), z: 8, core: 2. Of those that a mesh axis runs over, the one named last changes fastest.
Arguments:
- normalized_input: bfloat16 [4096, 16384], P(None, 'dp'), may hold values from -16 to 16
- quantized_weight_codes: bfloat16 [4096, 8, 128], P('dp', 'tensor'), may hold values from -0.09375 to 0.09375
- exponents: int32 [64, 8], P('dp', 'tensor'), may hold values from -2 to 1
- queries: bfloat16 [16384, 8, 512], P('dp', 'tensor'), may hold values from -64 to 64
- rotated_keys: bfloat16 [16384, 8, 128], P('dp', 'tensor'), may hold values from -4 to 4
- doc_start: int32 [16384], P('dp'), may hold values from 0 to 16383, as said below
- output_cotangent: bfloat16 [16384, 8, 512], P('dp', 'tensor'), may hold values from -6 to 6
Outputs:
- attention_output: bfloat16 [16384, 8, 512], P('dp', 'tensor')
- query_gradient: bfloat16 [16384, 8, 512], P('dp', 'tensor')
- d_keys: bfloat16 [16384, 8, 128], P('dp', 'tensor')
- d_input: bfloat16 [4096, 16384], P('tensor', 'dp')
- projection_gradient: float32 [4096, 8, 128], P('dp', 'tensor')
Inputs may be any that keep to these rules, and one draw needn't show every extreme that they name: doc_start[s] is the first position of the document holding token s: it never falls, doc_start[s] <= s, doc_start[doc_start[s]] = doc_start[s], and s - doc_start[s] <= 1023, with equality for some token in every draw.
All inputs are finite; a program needn't handle non-finite values.
Results may differ from a plain program's by a relative error of at most 0.017.
Values may be sent and summed in bfloat16 or wider, within the bound.
No kernel may reach another device: no remote copies, remote signals or barrier semaphores. Data moves between devices by JAX's collectives and lax.ppermute only.
A program may use at most 64 MiB of HBM per device.

v0:
```python
import math

import jax
import jax.numpy as jnp
import numpy as np
from jax import lax
from jax.sharding import PartitionSpec as P

SPAN = 4


powers_table = np.array([0.25, 0.5, 1.0, 2.0], dtype=np.float32)


def shifted(value, axis, steps):
    count = lax.axis_size(axis)
    first, last = (max(0, -steps), min(count, count - steps))
    return lax.ppermute(value, axis, [(source, source + steps) for source in range(first, last)])


def block_scale(exponents):
    levels = jnp.arange(4, dtype=jnp.int32) - 2
    picked = (exponents[..., None] == levels).astype(jnp.float32)
    return jnp.sum(picked * jnp.asarray(powers_table, dtype=jnp.float32), axis=-1)


def dequantize(quantized_weight_codes, exponents):
    scales = block_scale(exponents)
    repeat_rows = quantized_weight_codes.shape[0] // exponents.shape[0]
    row_scales = jnp.repeat(scales, repeat_rows, axis=0)
    return (quantized_weight_codes.astype(jnp.float32) * row_scales[:, :, None]).astype(
        jnp.bfloat16
    )


def attend(query_rows, key_window, value_window, grad_rows, query_pos, key_pos, first_pos):
    row_count, head_count, q_width = query_rows.shape
    head_size = key_window.shape[-1]
    group_size = q_width // head_size
    factor = 1.0 / math.sqrt(head_size)
    q_heads = query_rows.reshape(row_count, head_count, group_size, head_size)
    g_heads = grad_rows.reshape(row_count, head_count, group_size, head_size)
    scores = (
        jnp.einsum("thge,she->thgs", q_heads, key_window, preferred_element_type=jnp.float32)
        * factor
    )
    allowed = (key_pos[None, :] >= first_pos[:, None]) & (key_pos[None, :] <= query_pos[:, None])
    allowed = allowed[:, None, None, :]
    masked = jnp.where(allowed, scores, -1e30)
    row_top = jnp.max(masked, axis=-1, keepdims=True)
    row_total = jnp.sum(jnp.where(allowed, jnp.exp(masked - row_top), 0.0), axis=-1, keepdims=True)
    log_total = row_top + jnp.log(row_total)
    weights_bf = lax.optimization_barrier(
        jnp.where(allowed, jnp.exp(masked - log_total), 0.0).astype(jnp.bfloat16)
    )
    attn_rows = lax.optimization_barrier(
        jnp.einsum(
            "thgs,she->thge", weights_bf, value_window, preferred_element_type=jnp.float32
        ).astype(jnp.bfloat16)
    )
    row_delta = jnp.sum(
        g_heads.astype(jnp.float32) * attn_rows.astype(jnp.float32), axis=-1, keepdims=True
    )
    d_weights = jnp.einsum(
        "thge,she->thgs", g_heads, value_window, preferred_element_type=jnp.float32
    )
    d_scores = (weights_bf.astype(jnp.float32) * (d_weights - row_delta) * factor).astype(
        jnp.bfloat16
    )
    query_gradient = jnp.einsum(
        "thgs,she->thge", d_scores, key_window, preferred_element_type=jnp.float32
    ).astype(jnp.bfloat16)
    d_key = jnp.einsum("thgs,thge->she", d_scores, q_heads, preferred_element_type=jnp.float32)
    d_value = jnp.einsum("thgs,thge->she", weights_bf, g_heads, preferred_element_type=jnp.float32)
    return (
        attn_rows.reshape(row_count, head_count, q_width),
        query_gradient.reshape(row_count, head_count, q_width),
        d_key,
        d_value,
    )


def fetch_rows(weight_local):
    return lax.all_gather(weight_local, "dp", axis=0, tiled=True)


def body(
    normalized_input,
    quantized_weight_codes,
    exponents,
    queries,
    rotated_keys,
    doc_start,
    output_cotangent,
):
    feat_rows, tok_rows = normalized_input.shape
    local_heads = rotated_keys.shape[1]
    head_size = rotated_keys.shape[2]
    weight_local = dequantize(quantized_weight_codes, exponents)
    flattened_weight = fetch_rows(weight_local).reshape(feat_rows, local_heads * head_size)
    projected_values = lax.dot_general(
        normalized_input,
        flattened_weight,
        (((0,), (0,)), ((), ())),
        preferred_element_type=jnp.float32,
    )
    projected_values = projected_values.astype(jnp.bfloat16).reshape(
        tok_rows, local_heads, head_size
    )
    dp_index = lax.axis_index("dp")
    both_local = jnp.stack([rotated_keys, projected_values])
    earlier = [shifted(both_local, "dp", offset) for offset in range(1, SPAN + 1)]
    both_window = jnp.concatenate(earlier[::-1] + [both_local], axis=1)
    query_pos = dp_index * tok_rows + jnp.arange(tok_rows, dtype=jnp.int32)
    key_pos = (dp_index - SPAN) * tok_rows + jnp.arange((SPAN + 1) * tok_rows, dtype=jnp.int32)
    attention_output, query_gradient, d_key, d_value = attend(
        queries, both_window[0], both_window[1], output_cotangent, query_pos, key_pos, doc_start
    )
    grads_window = jnp.stack([d_key, d_value])

    def grad_piece(offset):
        begin_row = (SPAN - offset) * tok_rows
        return grads_window[:, begin_row : begin_row + tok_rows]

    grad_sum = grad_piece(0)
    for offset in range(1, SPAN + 1):
        grad_sum = grad_sum + shifted(grad_piece(offset), "dp", -offset)
    d_keys = grad_sum[0].astype(jnp.bfloat16)
    value_heads = grad_sum[1].astype(jnp.bfloat16)
    value_flat = value_heads.reshape(tok_rows, local_heads * head_size)
    backward_weight = fetch_rows(lax.optimization_barrier(weight_local)).reshape(
        feat_rows, local_heads * head_size
    )
    d_input = lax.psum_scatter(
        lax.dot_general(
            backward_weight,
            value_flat,
            (((1,), (1,)), ((), ())),
            preferred_element_type=jnp.float32,
        ).astype(jnp.bfloat16),
        "tensor",
        scatter_dimension=0,
        tiled=True,
    )
    w_flat = lax.psum_scatter(
        jnp.dot(normalized_input, value_flat, preferred_element_type=jnp.float32),
        "dp",
        scatter_dimension=0,
        tiled=True,
    )
    projection_gradient = w_flat.reshape(w_flat.shape[0], local_heads, head_size)
    return (attention_output, query_gradient, d_keys, d_input, projection_gradient)


def solution(mesh):
    in_specs = (
        P(None, "dp"),
        P("dp", "tensor", None),
        P("dp", "tensor"),
        P("dp", "tensor", None),
        P("dp", "tensor", None),
        P("dp"),
        P("dp", "tensor", None),
    )
    out_specs = (
        P("dp", "tensor", None),
        P("dp", "tensor", None),
        P("dp", "tensor", None),
        P("tensor", "dp"),
        P("dp", "tensor", None),
    )
    return jax.shard_map(body, mesh=mesh, in_specs=in_specs, out_specs=out_specs, check_vma=False)
```

profile of v0, /device:TPU:56, one launch (start us, length us, event | category | flops | bytes accessed | tf_op | source)
XLA Modules:
  0.0 989.0 jit_solution(8867303549016236233)
XLA Ops:
  8.0 1.3 fusion.35
  9.3 2.0 multiply_convert_fusion
  12.1 0.9 copy.26
  13.1 304.6 %all-gather.3.cloned.1.call-done = bf16[4096,1,128]{2,0,1:T(8,128)(2,1)} async-done(((bf16[64,1,128]{2,0,1:T(8,128)(2,1)}), bf16[4096,1,128]{2,0,1:T(8,128)(2,1)}) %all-gather.3.cloned.1.call-update) | async-done | bytes 1048592 | tf_op jit(solution)/shard_map/all_gather | solution.py:84
  317.7 1.8 fusion.16
  320.2 1.9 collective-permute-start
  322.1 1.9 collective-permute-start.1
  324.6 1.0 reshape.197
  325.6 1.9 collective-permute-start.2
  327.5 2.2 collective-permute-start.3
  329.8 7.5 collective-permute-done
  337.3 0.9 constant_dynamic-update-slice_fusion.4
  338.2 2.1 collective-permute-done.1
  340.3 0.9 constant_dynamic-update-slice_fusion.3
  341.2 0.9 collective-permute-done.3
  343.0 1.0 fusion.36
  344.0 1.0 select_reduce_fusion
  345.0 1.0 select_convert_fusion
  347.5 1.0 fusion.2
  350.1 1.9 collective-permute-start.4
  352.0 5.3 collective-permute-start.5
  357.3 5.2 collective-permute-start.6
  362.5 8.3 collective-permute-start.7
  370.8 1.9 collective-permute-done.6
  372.8 2.1 collective-permute-done.7
  375.0 2.2 convolution_bitcast_fusion
  377.2 2.9 copy.45
  380.2 241.6 %all-gather.5.cloned.1.call-done = bf16[4096,1,128]{2,0,1:T(8,128)(2,1)} async-done(((bf16[64,1,128]{2,0,1:T(8,128)(2,1)}), bf16[4096,1,128]{2,0,1:T(8,128)(2,1)}) %all-gather.5.cloned.1.call-update) | async-done | bytes 1048592 | tf_op jit(solution)/shard_map/all_gather | solution.py:84
  621.8 3.3 convolution_convert_fusion
  625.1 2.3 convolution_convert_fusion.1
  629.7 312.9 %reduce-scatter.7.cloned.1.call-done = f32[64,128]{1,0:T(8,128)} async-done(((f32[4096,128]{1,0:T(8,128)}), f32[64,128]{1,0:T(8,128)}) %reduce-scatter.7.cloned.1.call-update) | async-done | bytes 32784
  944.2 38.3 %reduce-scatter.5.cloned.1.call-done = bf16[512,256]{1,0:T(8,128)(2,1)} async-done(((bf16[4096,256]{1,0:T(8,128)(2,1)}), bf16[512,256]{1,0:T(8,128)(2,1)}) %reduce-scatter.5.cloned.1.call-update) | async-done | bytes 262160 | tf_op jit(solution)/shard_map/reduce_scatter | solution.py:134
  (50 shorter events, 10.0 us)
Async XLA Ops:
  7.2 310.5 %copy-start = (bf16[4096,256]{1,0:T(8,128)(2,1)S(1)}, bf16[4096,256]{1,0:T(8,128)(2,1)}, u32[]{:S(2)}) copy-start(bf16[4096,256]{1,0:T(8,128)(2,1)} %param.8) | copy-start | bytes 6291460
  7.2 316.8 %copy-start.8 = (s32[256]{0:T(256)S(1)}, s32[256]{0:T(256)}, u32[]{:S(2)}) copy-start(s32[256]{0:T(256)} %param.13) | copy-start | bytes 3076
  7.2 317.2 %copy-start.4 = (bf16[256,1,512]{2,0,1:T(8,128)(2,1)S(1)}, bf16[256,1,512]{2,0,1:T(8,128)(2,1)}, u32[]{:S(2)}) copy-start(bf16[256,1,512]{2,0,1:T(8,128)(2,1)} %param.14) | copy-start | bytes 786436
  7.2 310.5 %all-gather.3.cloned.1.call-start = ((), (), s32[]{:S(2)}) async-start(), calls=%async_computation.2 | async-start | bytes 1064960 | tf_op jit(solution)/shard_map/all_gather | solution.py:84
  11.3 610.5 %all-gather.5.cloned.1.call-start = ((), (), s32[]{:S(2)}) async-start(), calls=%async_computation.3 | async-start | bytes 1064960 | tf_op jit(solution)/shard_map/all_gather | solution.py:84
  12.1 930.5 %reduce-scatter.7.cloned.1.call-start = ((), (), s32[]{:S(2)}) async-start(), calls=%async_computation.5 | async-start | bytes 2129920
  13.1 311.3 %copy-start.7 = (bf16[256,1,128]{0,2,1:T(8,128)(2,1)}, bf16[256,1,128]{0,2,1:T(8,128)(2,1)S(1)}, u32[]{:S(2)}) copy-start(bf16[256,1,128]{0,2,1:T(8,128)(2,1)S(1)} %copy.26) | copy-start | bytes 196612
  320.2 17.1 %collective-permute-start = (bf16[2,256,1,128]{1,3,2,0:T(8,128)(2,1)}, bf16[2,256,1,128]{1,3,2,0:T(8,128)(2,1)}, u32[]{:S(2)}, u32[]{:S(2)}) collective-permute-start(bf16[2,256,1,128]{1,3,2,0:T(8,128)(2,1)} %pad_maximum_fusion.1), channel_id=1, source_target_pairs={{0,32},{8,40},{16,48},{24,56},{32,64},{40,72},{48,80},{56,88},{64,... | collective-permute-start | bytes 393224 | tf_op jit(solution)/shard_map/ppermute | solution.py:18
  322.1 18.2 %collective-permute-start.1 = (bf16[2,256,1,128]{1,3,2,0:T(8,128)(2,1)}, bf16[2,256,1,128]{1,3,2,0:T(8,128)(2,1)}, u32[]{:S(2)}, u32[]{:S(2)}) collective-permute-start(bf16[2,256,1,128]{1,3,2,0:T(8,128)(2,1)} %pad_maximum_fusion.1), channel_id=1, source_target_pairs={{0,24},{8,32},{16,40},{24,48},{32,56},{40,64},{48,72},{56,80},{64,... | collective-permute-start | bytes 393224 | tf_op jit(solution)/shard_map/ppermute | solution.py:18
  325.6 18.4 %copy-start.5 = (bf16[256,4,128]{2,1,0:T(4,128)(2,1)}, bf16[256,4,128]{2,1,0:T(4,128)(2,1)S(1)}, u32[]{:S(2)}) copy-start(bf16[256,4,128]{2,1,0:T(4,128)(2,1)S(1)} %reshape.197) | copy-start | bytes 786436
  325.6 15.6 %collective-permute-start.2 = (bf16[2,256,1,128]{1,3,2,0:T(8,128)(2,1)}, bf16[2,256,1,128]{1,3,2,0:T(8,128)(2,1)S(1)}, u32[]{:S(2)}, u32[]{:S(2)}) collective-permute-start(bf16[2,256,1,128]{1,3,2,0:T(8,128)(2,1)} %pad_maximum_fusion.1), channel_id=1, source_target_pairs={{0,16},{8,24},{16,32},{24,40},{32,48},{40,56},{48,64},{56,72},{64,... | collective-permute-start | bytes 393224 | tf_op jit(solution)/shard_map/ppermute | solution.py:18
  327.5 14.6 %collective-permute-start.3 = (bf16[2,256,1,128]{1,3,2,0:T(8,128)(2,1)}, bf16[2,256,1,128]{1,3,2,0:T(8,128)(2,1)S(1)}, u32[]{:S(2)}, u32[]{:S(2)}) collective-permute-start(bf16[2,256,1,128]{1,3,2,0:T(8,128)(2,1)} %pad_maximum_fusion.1), channel_id=1, source_target_pairs={{0,8},{8,16},{16,24},{24,32},{32,40},{40,48},{48,56},{56,64},{64,7... | collective-permute-start | bytes 393224 | tf_op jit(solution)/shard_map/ppermute | solution.py:18
  343.0 4.5 copy-start.2
  347.5 1.0 copy-start.6
  348.6 1.5 copy-start.1
  350.1 20.8 %collective-permute-start.4 = (f32[2,256,1,128]{3,1,2,0:T(8,128)S(1)}, f32[2,256,1,128]{3,1,2,0:T(8,128)S(1)}, u32[]{:S(2)}, u32[]{:S(2)}) collective-permute-start(f32[2,256,1,128]{3,1,2,0:T(8,128)S(1)} %get-tuple-element.15), channel_id=1, source_target_pairs={{8,0},{16,8},{24,16},{32,24},{40,32},{48,40},{56,48},{64,56},{72,6... | collective-permute-start | bytes 786440 | tf_op jit(solution)/shard_map/ppermute | solution.py:18
  352.0 18.9 %collective-permute-start.5 = (f32[2,256,1,128]{3,1,2,0:T(8,128)S(1)}, f32[2,256,1,128]{3,1,2,0:T(8,128)S(1)}, u32[]{:S(2)}, u32[]{:S(2)}) collective-permute-start(f32[2,256,1,128]{3,1,2,0:T(8,128)S(1)} %get-tuple-element.16), channel_id=1, source_target_pairs={{16,0},{24,8},{32,16},{40,24},{48,32},{56,40},{64,48},{72,56},{80,... | collective-permute-start | bytes 786440 | tf_op jit(solution)/shard_map/ppermute | solution.py:18
  357.3 15.5 %collective-permute-start.6 = (f32[2,256,1,128]{3,1,2,0:T(8,128)S(1)}, f32[2,256,1,128]{3,1,2,0:T(8,128)S(1)}, u32[]{:S(2)}, u32[]{:S(2)}) collective-permute-start(f32[2,256,1,128]{3,1,2,0:T(8,128)S(1)} %get-tuple-element.18), channel_id=1, source_target_pairs={{24,0},{32,8},{40,16},{48,24},{56,32},{64,40},{72,48},{80,56},{88,... | collective-permute-start | bytes 786440 | tf_op jit(solution)/shard_map/ppermute | solution.py:18
  362.5 12.4 %collective-permute-start.7 = (f32[2,256,1,128]{3,1,2,0:T(8,128)S(1)}, f32[2,256,1,128]{3,1,2,0:T(8,128)S(1)}, u32[]{:S(2)}, u32[]{:S(2)}) collective-permute-start(f32[2,256,1,128]{3,1,2,0:T(8,128)S(1)} %get-tuple-element.17), channel_id=1, source_target_pairs={{32,0},{40,8},{48,16},{56,24},{64,32},{72,40},{80,48},{88,56},{96,... | collective-permute-start | bytes 786440 | tf_op jit(solution)/shard_map/ppermute | solution.py:18
  380.1 245.0 %copy-start.3 = (bf16[2,1280,1,128]{1,3,2,0:T(8,128)(2,1)S(1)}, bf16[2,1280,1,128]{1,3,2,0:T(8,128)(2,1)}, u32[]{:S(2)}) copy-start(bf16[2,1280,1,128]{1,3,2,0:T(8,128)(2,1)} %copy-done.2) | copy-start | bytes 1966084
  380.1 602.3 %reduce-scatter.5.cloned.1.call-start = ((), (), s32[]{:S(2)}) async-start(), calls=%async_computation.4 | async-start | bytes 2359296 | tf_op jit(solution)/shard_map/reduce_scatter | solution.py:134
Sparse Core Ops, SparseCore 0:
  11.4 306.2 all-gather.2
  320.3 301.4 all-gather.4
  624.6 317.9 reduce-scatter.6
  946.1 36.2 reduce-scatter.4
where the time goes:
time: 995 us; the launch traced here: 989 us
  waiting for transfers between devices  913 us (92%)
  starting transfers between devices  28.9 us (3%)
  between operations  14.9 us (1%)
  matrix products  13.8 us (1%)
  local copies, waits for them, and re-layouts  11.4 us (1%)
    all_gather x2, waiting for transfers between devices, fetch_rows(): return lax.all_gather(weight_local, 'dp', axis=0, tiled=True)  546 us
    unnamed x5, waiting for transfers between devices  314 us
    reduce_scatter x1, waiting for transfers between devices, body(): lax.psum_scatter(lax.dot_general(backward_weight, value_flat, (((1,), (1,...  38.3 us
    ppermute x8, starting transfers between devices, shifted(): lax.ppermute(value, axis, [(source, source + steps) for source in range(f...  28.7 us
  transfers between devices with their start and end apart: 12, of which 9 were waited for; matrix products, arithmetic and copies ran while one was open for 3% of the time, Pallas kernels for 0%

commit v1 on v0

v1 whole, which is shorter than its diff:
```python
import math

import jax
import jax.numpy as jnp
import numpy as np
from jax import lax
from jax.sharding import PartitionSpec as P

SPAN = 4
Z = 8
YX = 8
F32 = jnp.float32
BF16 = jnp.bfloat16

powers_table = np.array([0.25, 0.5, 1.0, 2.0], dtype=np.float32)

Z_GROUPS = [[a * Z + z for z in range(Z)] for a in range(YX)]
YX_GROUPS = [[a * Z + z for a in range(YX)] for z in range(Z)]


def shifted(value, steps):
    count = lax.axis_size("dp")
    first, last = (max(0, -steps), min(count, count - steps))
    return lax.ppermute(value, "dp", [(source, source + steps) for source in range(first, last)])


def swap_all(value, groups):
    return lax.all_to_all(value, "dp", 0, 0, tiled=True, axis_index_groups=groups)


def copies(value, count):
    return jnp.broadcast_to(value[None], (count,) + value.shape).reshape(
        (count * value.shape[0],) + value.shape[1:]
    )


def dequantize(codes, exponent):
    levels = jnp.arange(4, dtype=jnp.int32) - 2
    scale = jnp.sum((exponent == levels).astype(F32) * jnp.asarray(powers_table))
    return (codes.astype(F32) * scale).astype(BF16)


def transposed_heads(value):
    pairs = []
    for a in range(YX):
        for z in range(Z):
            for h in range(8):
                pairs.append(((a * Z + z) * 8 + h, (h * Z + z) * 8 + a))
    return lax.ppermute(value, ("dp", "tensor"), pairs)


def body(x, codes, exponents, queries, keys, doc_start, cotangent):
    feat, tok = x.shape
    width = keys.shape[2]
    group = queries.shape[2] // width
    factor = 1.0 / math.sqrt(width)
    dp_index = lax.axis_index("dp")

    key_own = keys[:, 0, :]
    w_own = dequantize(codes[:, 0, :], exponents[0, 0])
    w_block = swap_all(copies(w_own, Z), Z_GROUPS)
    w_swapped = transposed_heads(w_own)

    def window(own, halo):
        return jnp.concatenate(halo[::-1] + [own], axis=0)

    key_window = window(key_own, [shifted(key_own, s) for s in range(1, SPAN + 1)])
    w_full = swap_all(copies(w_block, YX), YX_GROUPS)

    def rows_of(arr):
        return jnp.concatenate(
            [arr[:, 0, g * width : (g + 1) * width] for g in range(group)], axis=0
        )

    def lanes_of(arr):
        return jnp.concatenate([arr[g * tok : (g + 1) * tok] for g in range(group)], axis=1)[
            :, None, :
        ]

    q_rows = rows_of(queries)
    g_rows = rows_of(cotangent)
    query_pos = dp_index * tok + jnp.arange(tok, dtype=jnp.int32)
    key_pos = (dp_index - SPAN) * tok + jnp.arange((SPAN + 1) * tok, dtype=jnp.int32)
    allowed = (key_pos[None, :] >= doc_start[:, None]) & (key_pos[None, :] <= query_pos[:, None])

    scores = lax.dot_general(
        q_rows, key_window, (((1,), (1,)), ((), ())), preferred_element_type=F32
    ).reshape(group, tok, -1)
    masked = jnp.where(allowed[None], scores * factor, -1e30)
    row_top = jnp.max(masked, axis=-1, keepdims=True)
    row_total = jnp.sum(jnp.exp(masked - row_top), axis=-1, keepdims=True)
    log_total = row_top + jnp.log(row_total)
    probs = jnp.exp(masked - log_total).astype(BF16).reshape(group * tok, -1)
    dv_window = lax.dot_general(
        probs, g_rows, (((0,), (0,)), ((), ())), preferred_element_type=F32
    )

    def halo_sum(grads):
        def piece(offset):
            begin = (SPAN - offset) * tok
            return grads[begin : begin + tok]

        total = piece(0)
        for offset in range(1, SPAN + 1):
            total = total + shifted(piece(offset).astype(BF16), -offset).astype(F32)
        return total.astype(BF16)

    dv_own = halo_sum(dv_window)

    v_own = lax.dot_general(
        x, w_full, (((0,), (0,)), ((), ())), preferred_element_type=F32
    ).astype(BF16)
    value_window = window(v_own, [shifted(v_own, s) for s in range(1, SPAN + 1)])

    dw_part = lax.dot_general(
        x, dv_own, (((1,), (0,)), ((), ())), preferred_element_type=F32
    ).astype(BF16)
    dw_block = swap_all(dw_part, YX_GROUPS).reshape(YX, feat // YX, width)
    dw_block = jnp.sum(dw_block.astype(F32), axis=0).astype(BF16)
    dw_own = swap_all(dw_block, Z_GROUPS).reshape(Z, feat // (YX * Z), width)
    projection_gradient = jnp.sum(dw_own.astype(F32), axis=0)[:, None, :]

    w_rows = swap_all(copies(swap_all(copies(w_swapped, Z), Z_GROUPS), YX), YX_GROUPS)
    w_rows = w_rows.reshape(8, feat // 8, width)
    dv_heads = lax.all_to_all(copies(dv_own, 8), "tensor", 0, 0, tiled=True)
    dv_heads = dv_heads.reshape(8, tok, width)
    d_input = jnp.zeros((feat // 8, tok), F32)
    for h in range(8):
        d_input = d_input + lax.dot_general(
            w_rows[h], dv_heads[h], (((1,), (1,)), ((), ())), preferred_element_type=F32
        )
    d_input = d_input.astype(BF16)

    attn = lax.dot_general(
        probs, value_window, (((1,), (0,)), ((), ())), preferred_element_type=F32
    ).astype(BF16)
    delta = jnp.sum(g_rows.astype(F32) * attn.astype(F32), axis=-1, keepdims=True)
    dprob = lax.dot_general(
        g_rows, value_window, (((1,), (1,)), ((), ())), preferred_element_type=F32
    )
    dscore = (probs.astype(F32) * (dprob - delta) * factor).astype(BF16)
    dq = lax.dot_general(
        dscore, key_window, (((1,), (0,)), ((), ())), preferred_element_type=F32
    ).astype(BF16)
    dk_window = lax.dot_general(
        dscore, q_rows, (((0,), (0,)), ((), ())), preferred_element_type=F32
    )
    d_keys = halo_sum(dk_window)[:, None, :]
    return (lanes_of(attn), lanes_of(dq), d_keys, d_input, projection_gradient)


def solution(mesh):
    in_specs = (
        P(None, "dp"),
        P("dp", "tensor", None),
        P("dp", "tensor"),
        P("dp", "tensor", None),
        P("dp", "tensor", None),
        P("dp"),
        P("dp", "tensor", None),
    )
    out_specs = (
        P("dp", "tensor", None),
        P("dp", "tensor", None),
        P("dp", "tensor", None),
        P("tensor", "dp"),
        P("dp", "tensor", None),
    )
    return jax.shard_map(body, mesh=mesh, in_specs=in_specs, out_specs=out_specs, check_vma=False)
```

time: 995 us -> 226 us (0.23)
  waiting for transfers between devices: 913 us -> 27.1 us
  starting transfers between devices: 28.9 us -> 108 us
  blocking collectives: 0 us -> 34.8 us
  between operations: 14.9 us -> 1.99 us
    all_gather x2 -> x0, waiting for transfers between devices: 546 us -> none  [fetch_rows(): return lax.all_gather(weight_local, 'dp', axis=0, tiled=True)]
    unnamed x5 -> x0, waiting for transfers between devices: 314 us -> none
    ppermute x8 -> x17, starting transfers between devices: 28.7 us -> 81.1 us  [the longest x16 77.6 us: shifted(): lax.ppermute(value, 'dp', [(source, source + steps) for source in range(f...]
    reduce_scatter x1 -> x0, waiting for transfers between devices: 38.3 us -> none  [body(): lax.psum_scatter(lax.dot_general(backward_weight, value_flat, (((1,), (1,...]
    all_to_all x0 -> x2, blocking collectives: none -> 34.8 us  [swap_all(): lax.all_to_all(value, 'dp', 0, 0, tiled=True, axis_index_groups=groups)]
    all_to_all x0 -> x5, starting transfers between devices: none -> 26.8 us  [the longest x4 21.4 us: swap_all(): lax.all_to_all(value, 'dp', 0, 0, tiled=True, axis_index_groups=groups)]
    all_to_all x0 -> x5, waiting for transfers between devices: none -> 21.5 us  [the longest x1 13.5 us: body(): dv_heads = lax.all_to_all(copies(dv_own, 8), 'tensor', 0, 0, tiled=True)]
  transfers between devices with their start and end apart: 12 -> 22, of which waited for: 9 -> 3; matrix products, arithmetic and copies ran while one was open for 3% -> 21% of each run, Pallas kernels for 0% -> 0%
where the time goes in v1:
time: 226 us; the launch traced here: 222 us
  starting transfers between devices  108 us (48%)
  blocking collectives  34.8 us (15%)
  waiting for transfers between devices  27.1 us (12%)
  local copies, waits for them, and re-layouts  20.7 us (9%)
  matrix products  18.6 us (8%)
  other arithmetic  11 us (5%)
    ppermute x16, starting transfers between devices, shifted(): lax.ppermute(value, 'dp', [(source, source + steps) for source in range(f...  77.6 us
    all_to_all x2, blocking collectives, swap_all(): lax.all_to_all(value, 'dp', 0, 0, tiled=True, axis_index_groups=groups)  34.8 us
    all_to_all x4, starting transfers between devices, swap_all(): lax.all_to_all(value, 'dp', 0, 0, tiled=True, axis_index_groups=groups)  21.4 us
    all_to_all x1, waiting for transfers between devices, body(): dv_heads = lax.all_to_all(copies(dv_own, 8), 'tensor', 0, 0, tiled=True)  13.5 us
    unnamed x54, local copies, waits for them, and re-layouts  9.56 us
    dot_general x8, matrix products, body(): lax.dot_general(w_rows[h], dv_heads[h], (((1,), (1,)), ((), ())), preferr...  9.37 us
    all_to_all x4, waiting for transfers between devices, swap_all(): lax.all_to_all(value, 'dp', 0, 0, tiled=True, axis_index_groups=groups)  8.03 us
    ppermute x1, waiting for transfers between devices, transposed_heads(): return lax.ppermute(value, ('dp', 'tensor'), pairs)  5.54 us
  transfers between devices with their start and end apart: 22, of which 3 were waited for; matrix products, arithmetic and copies ran while one was open for 21% of the time, Pallas kernels for 0%

profile of v1, /device:TPU:56, one launch (start us, length us, event | category | flops | bytes accessed | tf_op | source)
XLA Modules:
  0.0 222.2 jit_solution(5352575832222684900)
XLA Ops:
  0.6 11.1 %collective-permute-start = (bf16[256,128]{1,0:T(8,128)(2,1)}, bf16[256,128]{1,0:T(8,128)(2,1)}, u32[]{:S(2)}, u32[]{:S(2)}) collective-permute-start(bf16[256,128]{1,0:T(8,128)(2,1)} %bitcast.116), channel_id=1, source_target_pairs={{0,32},{8,40},{16,48},{24,56},{32,64},{40,72},{48,80},{56,88},{64,... | collective-permute-start | bytes 196616 | tf_op jit(solution)/shard_map/ppermute | solution.py:24
  11.7 5.2 %collective-permute-start.1 = (bf16[256,128]{1,0:T(8,128)(2,1)}, bf16[256,128]{1,0:T(8,128)(2,1)}, u32[]{:S(2)}, u32[]{:S(2)}) collective-permute-start(bf16[256,128]{1,0:T(8,128)(2,1)} %bitcast.117), channel_id=1, source_target_pairs={{0,24},{8,32},{16,40},{24,48},{32,56},{40,64},{48,72},{56,80},{64,... | collective-permute-start | bytes 196616 | tf_op jit(solution)/shard_map/ppermute | solution.py:24
  16.9 1.9 collective-permute-start.2
  18.8 2.5 %collective-permute-start.3 = (bf16[256,128]{1,0:T(8,128)(2,1)}, bf16[256,128]{1,0:T(8,128)(2,1)}, u32[]{:S(2)}, u32[]{:S(2)}) collective-permute-start(bf16[256,128]{1,0:T(8,128)(2,1)} %bitcast.119), channel_id=1, source_target_pairs={{0,8},{8,16},{16,24},{24,32},{32,40},{40,48},{48,56},{56,64},{64,7... | collective-permute-start | bytes 196616 | tf_op jit(solution)/shard_map/ppermute | solution.py:24
  25.3 7.2 %all-to-all-start = ((bf16[8,64,128]{2,1,0:T(8,128)(2,1)}), bf16[8,64,128]{2,1,0:T(8,128)(2,1)S(1)}, u32[]{:S(2)}, u32[]{:S(2)}) async-start(bf16[8,64,128]{2,1,0:T(8,128)(2,1)} %broadcast_in_dim.39), calls=%async_computation | async-start | bytes 262144 | tf_op jit(solution)/shard_map/all_to_all | solution.py:28
  45.9 7.2 %collective-permute-start.13 = (bf16[256,128]{1,0:T(8,128)(2,1)}, bf16[256,128]{1,0:T(8,128)(2,1)S(1)}, u32[]{:S(2)}, u32[]{:S(2)}) collective-permute-start(bf16[256,128]{1,0:T(8,128)(2,1)} %get-tuple-element.20), channel_id=1, source_target_pairs={{8,0},{16,8},{24,16},{32,24},{40,32},{48,40},{56,48},{64,56},{72,6... | collective-permute-start | bytes 196616 | tf_op jit(solution)/shard_map/ppermute | solution.py:24
  53.1 4.3 %collective-permute-start.14 = (bf16[256,128]{1,0:T(8,128)(2,1)}, bf16[256,128]{1,0:T(8,128)(2,1)S(1)}, u32[]{:S(2)}, u32[]{:S(2)}) collective-permute-start(bf16[256,128]{1,0:T(8,128)(2,1)} %get-tuple-element.23), channel_id=1, source_target_pairs={{16,0},{24,8},{32,16},{40,24},{48,32},{56,40},{64,48},{72,56},{80,... | collective-permute-start | bytes 196616 | tf_op jit(solution)/shard_map/ppermute | solution.py:24
  57.4 3.4 %collective-permute-start.15 = (bf16[256,128]{1,0:T(8,128)(2,1)}, bf16[256,128]{1,0:T(8,128)(2,1)}, u32[]{:S(2)}, u32[]{:S(2)}) collective-permute-start(bf16[256,128]{1,0:T(8,128)(2,1)} %get-tuple-element.22), channel_id=1, source_target_pairs={{24,0},{32,8},{40,16},{48,24},{56,32},{64,40},{72,48},{80,56},{88,... | collective-permute-start | bytes 196616 | tf_op jit(solution)/shard_map/ppermute | solution.py:24
  60.8 6.4 %collective-permute-start.16 = (bf16[256,128]{1,0:T(8,128)(2,1)}, bf16[256,128]{1,0:T(8,128)(2,1)}, u32[]{:S(2)}, u32[]{:S(2)}) collective-permute-start(bf16[256,128]{1,0:T(8,128)(2,1)} %get-tuple-element.21), channel_id=1, source_target_pairs={{32,0},{40,8},{48,16},{56,24},{64,32},{72,40},{80,48},{88,56},{96,... | collective-permute-start | bytes 196616 | tf_op jit(solution)/shard_map/ppermute | solution.py:24
  67.1 3.5 %collective-permute-start.12 = (bf16[64,128]{1,0:T(8,128)(2,1)S(1)}, bf16[64,128]{1,0:T(8,128)(2,1)S(1)}, u32[]{:S(2)}, u32[]{:S(2)}) collective-permute-start(bf16[64,128]{1,0:T(8,128)(2,1)S(1)} %fusion.13), channel_id=1, source_target_pairs={{0,0},{1,64},{2,128},{3,192},{4,256},{5,320},{6,384},{7,448},{8,8}... | collective-permute-start | bytes 49160 | tf_op jit(solution)/shard_map/ppermute | solution.py:49
  70.6 5.5 %collective-permute-done.12 = bf16[64,128]{1,0:T(8,128)(2,1)S(1)} collective-permute-done((bf16[64,128]{1,0:T(8,128)(2,1)S(1)}, bf16[64,128]{1,0:T(8,128)(2,1)S(1)}, u32[]{:S(2)}, u32[]{:S(2)}) %collective-permute-start.12) | collective-permute-done | bytes 16416 | tf_op jit(solution)/shard_map/ppermute | solution.py:49
  76.9 3.4 %all-to-all-start.2 = ((bf16[8,64,128]{2,1,0:T(8,128)(2,1)}), bf16[8,64,128]{2,1,0:T(8,128)(2,1)S(1)}, u32[]{:S(2)}, u32[]{:S(2)}) async-start(bf16[8,64,128]{2,1,0:T(8,128)(2,1)} %broadcast_in_dim.77), calls=%async_computation.2 | async-start | bytes 262144 | tf_op jit(solution)/shard_map/all_to_all | solution.py:28
  81.2 8.0 %all-to-all-done.2 = bf16[8,64,128]{2,1,0:T(8,128)(2,1)S(1)} async-done(((bf16[8,64,128]{2,1,0:T(8,128)(2,1)}), bf16[8,64,128]{2,1,0:T(8,128)(2,1)S(1)}, u32[]{:S(2)}, u32[]{:S(2)}) %all-to-all-start.2) | async-done | bytes 131104 | tf_op jit(solution)/shard_map/all_to_all | solution.py:28
  90.1 5.4 %all-to-all-start.4 = ((bf16[8,256,128]{2,1,0:T(8,128)(2,1)}), bf16[8,256,128]{2,1,0:T(8,128)(2,1)}, u32[]{:S(2)}, u32[]{:S(2)}) async-start(bf16[8,256,128]{2,1,0:T(8,128)(2,1)} %broadcast_in_dim.80), calls=%async_computation.4 | async-start | bytes 1048576 | tf_op jit(solution)/shard_map/all_to_all | solution.py:125
  96.5 13.5 %all-to-all-done.4 = bf16[8,256,128]{2,1,0:T(8,128)(2,1)} async-done(((bf16[8,256,128]{2,1,0:T(8,128)(2,1)}), bf16[8,256,128]{2,1,0:T(8,128)(2,1)}, u32[]{:S(2)}, u32[]{:S(2)}) %all-to-all-start.4) | async-done | bytes 524320 | tf_op jit(solution)/shard_map/all_to_all | solution.py:125
  110.0 18.3 %all_to_all.51 = bf16[8,512,128]{1,2,0:T(8,128)(2,1)} all-to-all(bf16[8,512,128]{1,2,0:T(8,128)(2,1)S(1)} %bitcast.100), channel_id=1, replica_groups={{0,64,128,192,256,320,384,448},{8,72,136,200,264,328,392,456},{16,80,14..., dimensions={0} | all-to-all | bytes 2097152 | tf_op jit(solution)/shard_map/all_to_all | solution.py:28
  129.3 16.5 %all_to_all.52 = bf16[8,512,128]{2,1,0:T(8,128)(2,1)} all-to-all(bf16[8,512,128]{2,1,0:T(8,128)(2,1)S(1)} %broadcast_in_dim.73), channel_id=1, replica_groups={{0,64,128,192,256,320,384,448},{8,72,136,200,264,328,392,456},{16,80,14..., dimensions={0} | all-to-all | bytes 2097152 | tf_op jit(solution)/shard_map/all_to_all | solution.py:28
  147.0 4.9 %all-to-all-start.3 = ((bf16[8,512,128]{2,1,0:T(8,128)(2,1)}), bf16[8,512,128]{2,1,0:T(8,128)(2,1)S(1)}, u32[]{:S(2)}, u32[]{:S(2)}) async-start(bf16[8,512,128]{2,1,0:T(8,128)(2,1)} %broadcast_in_dim.79), calls=%async_computation.3 | async-start | bytes 2097152 | tf_op jit(solution)/shard_map/all_to_all | solution.py:28
  151.8 2.1 reduce_sum.51
  153.9 1.7 copy.33
  155.6 2.4 %fusion.1 = bf16[256,128]{0,1:T(8,128)(2,1)} fusion(bf16[4096,128]{1,0:T(8,128)(2,1)} %bitcast.98, bf16[4096,256]{1,0:T(8,128)(2,1)S(1)} %copy-done), kind=kOutput, calls=%fused_computation.17 | convolution fusion | flops 268468224 | bytes 3211264 | tf_op jit(solution)/shard_map/dot_general | solution.py:110
  158.0 2.5 %collective-permute-start.4 = (bf16[256,128]{0,1:T(8,128)(2,1)}, bf16[256,128]{0,1:T(8,128)(2,1)}, u32[]{:S(2)}, u32[]{:S(2)}) collective-permute-start(bf16[256,128]{0,1:T(8,128)(2,1)} %fusion.1), channel_id=1, source_target_pairs={{0,32},{8,40},{16,48},{24,56},{32,64},{40,72},{48,80},{56,88},{64,... | collective-permute-start | bytes 196616 | tf_op jit(solution)/shard_map/ppermute | solution.py:24
  160.5 4.4 %collective-permute-start.5 = (bf16[256,128]{0,1:T(8,128)(2,1)}, bf16[256,128]{0,1:T(8,128)(2,1)}, u32[]{:S(2)}, u32[]{:S(2)}) collective-permute-start(bf16[256,128]{0,1:T(8,128)(2,1)} %fusion.1), channel_id=1, source_target_pairs={{0,24},{8,32},{16,40},{24,48},{32,56},{40,64},{48,72},{56,80},{64,... | collective-permute-start | bytes 196616 | tf_op jit(solution)/shard_map/ppermute | solution.py:24
  164.9 6.2 %collective-permute-start.6 = (bf16[256,128]{0,1:T(8,128)(2,1)}, bf16[256,128]{0,1:T(8,128)(2,1)}, u32[]{:S(2)}, u32[]{:S(2)}) collective-permute-start(bf16[256,128]{0,1:T(8,128)(2,1)} %fusion.1), channel_id=1, source_target_pairs={{0,16},{8,24},{16,32},{24,40},{32,48},{40,56},{48,64},{56,72},{64,... | collective-permute-start | bytes 196616 | tf_op jit(solution)/shard_map/ppermute | solution.py:24
  171.1 2.3 %collective-permute-start.7 = (bf16[256,128]{0,1:T(8,128)(2,1)}, bf16[256,128]{0,1:T(8,128)(2,1)}, u32[]{:S(2)}, u32[]{:S(2)}) collective-permute-start(bf16[256,128]{0,1:T(8,128)(2,1)} %fusion.1), channel_id=1, source_target_pairs={{0,8},{8,16},{16,24},{24,32},{32,40},{40,48},{48,56},{56,64},{64,7... | collective-permute-start | bytes 196616 | tf_op jit(solution)/shard_map/ppermute | solution.py:24
  173.4 5.9 %all-to-all-start.6 = ((bf16[8,64,128]{2,1,0:T(8,128)(2,1)}), bf16[8,64,128]{2,1,0:T(8,128)(2,1)}, u32[]{:S(2)}, u32[]{:S(2)}) async-start(bf16[8,64,128]{2,1,0:T(8,128)(2,1)} %bitcast.103), calls=%async_computation.6 | async-start | bytes 262144 | tf_op jit(solution)/shard_map/all_to_all | solution.py:28
  187.1 1.8 fusion
  197.8 9.0 %collective-permute-start.10 = (bf16[256,128]{1,0:T(8,128)(2,1)}, bf16[256,128]{1,0:T(8,128)(2,1)S(1)}, u32[]{:S(2)}, u32[]{:S(2)}) collective-permute-start(bf16[256,128]{1,0:T(8,128)(2,1)} %get-tuple-element.26), channel_id=1, source_target_pairs={{24,0},{32,8},{40,16},{48,24},{56,32},{64,40},{72,48},{80,56},{88,... | collective-permute-start | bytes 196616 | tf_op jit(solution)/shard_map/ppermute | solution.py:24
  206.9 3.4 %collective-permute-start.11 = (bf16[256,128]{1,0:T(8,128)(2,1)}, bf16[256,128]{1,0:T(8,128)(2,1)S(1)}, u32[]{:S(2)}, u32[]{:S(2)}) collective-permute-start(bf16[256,128]{1,0:T(8,128)(2,1)} %get-tuple-element.25), channel_id=1, source_target_pairs={{32,0},{40,8},{48,16},{56,24},{64,32},{72,40},{80,48},{88,56},{96,... | collective-permute-start | bytes 196616 | tf_op jit(solution)/shard_map/ppermute | solution.py:24
  210.3 1.9 collective-permute-start.8
  212.2 6.0 %collective-permute-start.9 = (bf16[256,128]{1,0:T(8,128)(2,1)}, bf16[256,128]{1,0:T(8,128)(2,1)S(1)}, u32[]{:S(2)}, u32[]{:S(2)}) collective-permute-start(bf16[256,128]{1,0:T(8,128)(2,1)} %get-tuple-element.27), channel_id=1, source_target_pairs={{16,0},{24,8},{32,16},{40,24},{48,32},{56,40},{64,48},{72,56},{80,... | collective-permute-start | bytes 196616 | tf_op jit(solution)/shard_map/ppermute | solution.py:24
  220.0 1.5 convert_reduce_fusion
  (113 shorter events, 41.0 us)
Async XLA Ops:
  0.6 94.9 %copy-start = (bf16[4096,256]{1,0:T(8,128)(2,1)S(1)}, bf16[4096,256]{1,0:T(8,128)(2,1)}, u32[]{:S(2)}) copy-start(bf16[4096,256]{1,0:T(8,128)(2,1)} %param.8) | copy-start | bytes 6291460
  0.6 35.4 %collective-permute-start = (bf16[256,128]{1,0:T(8,128)(2,1)}, bf16[256,128]{1,0:T(8,128)(2,1)}, u32[]{:S(2)}, u32[]{:S(2)}) collective-permute-start(bf16[256,128]{1,0:T(8,128)(2,1)} %bitcast.116), channel_id=1, source_target_pairs={{0,32},{8,40},{16,48},{24,56},{32,64},{40,72},{48,80},{56,88},{64,... | collective-permute-start | bytes 196616 | tf_op jit(solution)/shard_map/ppermute | solution.py:24
  11.7 25.2 %collective-permute-start.1 = (bf16[256,128]{1,0:T(8,128)(2,1)}, bf16[256,128]{1,0:T(8,128)(2,1)}, u32[]{:S(2)}, u32[]{:S(2)}) collective-permute-start(bf16[256,128]{1,0:T(8,128)(2,1)} %bitcast.117), channel_id=1, source_target_pairs={{0,24},{8,32},{16,40},{24,48},{32,56},{40,64},{48,72},{56,80},{64,... | collective-permute-start | bytes 196616 | tf_op jit(solution)/shard_map/ppermute | solution.py:24
  16.9 20.9 %collective-permute-start.2 = (bf16[256,128]{1,0:T(8,128)(2,1)}, bf16[256,128]{1,0:T(8,128)(2,1)}, u32[]{:S(2)}, u32[]{:S(2)}) collective-permute-start(bf16[256,128]{1,0:T(8,128)(2,1)} %bitcast.118), channel_id=1, source_target_pairs={{0,16},{8,24},{16,32},{24,40},{32,48},{40,56},{48,64},{56,72},{64,... | collective-permute-start | bytes 196616 | tf_op jit(solution)/shard_map/ppermute | solution.py:24
  18.8 19.8 %collective-permute-start.3 = (bf16[256,128]{1,0:T(8,128)(2,1)}, bf16[256,128]{1,0:T(8,128)(2,1)}, u32[]{:S(2)}, u32[]{:S(2)}) collective-permute-start(bf16[256,128]{1,0:T(8,128)(2,1)} %bitcast.119), channel_id=1, source_target_pairs={{0,8},{8,16},{16,24},{24,32},{32,40},{40,48},{48,56},{56,64},{64,7... | collective-permute-start | bytes 196616 | tf_op jit(solution)/shard_map/ppermute | solution.py:24
  25.3 50.9 %all-to-all-start = ((bf16[8,64,128]{2,1,0:T(8,128)(2,1)}), bf16[8,64,128]{2,1,0:T(8,128)(2,1)S(1)}, u32[]{:S(2)}, u32[]{:S(2)}) async-start(bf16[8,64,128]{2,1,0:T(8,128)(2,1)} %broadcast_in_dim.39), calls=%async_computation | async-start | bytes 262144 | tf_op jit(solution)/shard_map/all_to_all | solution.py:28
  33.5 8.1 %copy-start.3 = (bf16[256,128]{1,0:T(8,128)(2,1)}, bf16[256,128]{1,0:T(8,128)(2,1)S(1)}, u32[]{:S(2)}) copy-start(bf16[256,128]{1,0:T(8,128)(2,1)S(1)} %get-tuple-element.41) | copy-start | bytes 196612
  33.5 8.1 %copy-start.5 = (bf16[256,128]{1,0:T(8,128)(2,1)}, bf16[256,128]{1,0:T(8,128)(2,1)S(1)}, u32[]{:S(2)}) copy-start(bf16[256,128]{1,0:T(8,128)(2,1)S(1)} %get-tuple-element.42) | copy-start | bytes 196612
  33.5 8.1 %copy-start.7 = (bf16[256,128]{1,0:T(8,128)(2,1)}, bf16[256,128]{1,0:T(8,128)(2,1)S(1)}, u32[]{:S(2)}) copy-start(bf16[256,128]{1,0:T(8,128)(2,1)S(1)} %get-tuple-element.43) | copy-start | bytes 196612
  45.9 34.4 %collective-permute-start.13 = (bf16[256,128]{1,0:T(8,128)(2,1)}, bf16[256,128]{1,0:T(8,128)(2,1)S(1)}, u32[]{:S(2)}, u32[]{:S(2)}) collective-permute-start(bf16[256,128]{1,0:T(8,128)(2,1)} %get-tuple-element.20), channel_id=1, source_target_pairs={{8,0},{16,8},{24,16},{32,24},{40,32},{48,40},{56,48},{64,56},{72,6... | collective-permute-start | bytes 196616 | tf_op jit(solution)/shard_map/ppermute | solution.py:24
  53.1 27.2 %collective-permute-start.14 = (bf16[256,128]{1,0:T(8,128)(2,1)}, bf16[256,128]{1,0:T(8,128)(2,1)S(1)}, u32[]{:S(2)}, u32[]{:S(2)}) collective-permute-start(bf16[256,128]{1,0:T(8,128)(2,1)} %get-tuple-element.23), channel_id=1, source_target_pairs={{16,0},{24,8},{32,16},{40,24},{48,32},{56,40},{64,48},{72,56},{80,... | collective-permute-start | bytes 196616 | tf_op jit(solution)/shard_map/ppermute | solution.py:24
  57.4 22.9 %collective-permute-start.15 = (bf16[256,128]{1,0:T(8,128)(2,1)}, bf16[256,128]{1,0:T(8,128)(2,1)}, u32[]{:S(2)}, u32[]{:S(2)}) collective-permute-start(bf16[256,128]{1,0:T(8,128)(2,1)} %get-tuple-element.22), channel_id=1, source_target_pairs={{24,0},{32,8},{40,16},{48,24},{56,32},{64,40},{72,48},{80,56},{88,... | collective-permute-start | bytes 196616 | tf_op jit(solution)/shard_map/ppermute | solution.py:24
  60.8 19.5 %collective-permute-start.16 = (bf16[256,128]{1,0:T(8,128)(2,1)}, bf16[256,128]{1,0:T(8,128)(2,1)}, u32[]{:S(2)}, u32[]{:S(2)}) collective-permute-start(bf16[256,128]{1,0:T(8,128)(2,1)} %get-tuple-element.21), channel_id=1, source_target_pairs={{32,0},{40,8},{48,16},{56,24},{64,32},{72,40},{80,48},{88,56},{96,... | collective-permute-start | bytes 196616 | tf_op jit(solution)/shard_map/ppermute | solution.py:24
  67.1 9.0 %collective-permute-start.12 = (bf16[64,128]{1,0:T(8,128)(2,1)S(1)}, bf16[64,128]{1,0:T(8,128)(2,1)S(1)}, u32[]{:S(2)}, u32[]{:S(2)}) collective-permute-start(bf16[64,128]{1,0:T(8,128)(2,1)S(1)} %fusion.13), channel_id=1, source_target_pairs={{0,0},{1,64},{2,128},{3,192},{4,256},{5,320},{6,384},{7,448},{8,8}... | collective-permute-start | bytes 49160 | tf_op jit(solution)/shard_map/ppermute | solution.py:49
  76.9 12.4 %all-to-all-start.2 = ((bf16[8,64,128]{2,1,0:T(8,128)(2,1)}), bf16[8,64,128]{2,1,0:T(8,128)(2,1)S(1)}, u32[]{:S(2)}, u32[]{:S(2)}) async-start(bf16[8,64,128]{2,1,0:T(8,128)(2,1)} %broadcast_in_dim.77), calls=%async_computation.2 | async-start | bytes 262144 | tf_op jit(solution)/shard_map/all_to_all | solution.py:28
  90.1 19.8 %all-to-all-start.4 = ((bf16[8,256,128]{2,1,0:T(8,128)(2,1)}), bf16[8,256,128]{2,1,0:T(8,128)(2,1)}, u32[]{:S(2)}, u32[]{:S(2)}) async-start(bf16[8,256,128]{2,1,0:T(8,128)(2,1)} %broadcast_in_dim.80), calls=%async_computation.4 | async-start | bytes 1048576 | tf_op jit(solution)/shard_map/all_to_all | solution.py:125
  110.0 35.9 %copy-start.11 = (bf16[8,64,128]{2,1,0:T(8,128)(2,1)S(1)}, bf16[8,64,128]{2,1,0:T(8,128)(2,1)}, u32[]{:S(2)}) copy-start(bf16[8,64,128]{2,1,0:T(8,128)(2,1)} %copy-done.10) | copy-start | bytes 393220
  147.0 26.5 %all-to-all-start.3 = ((bf16[8,512,128]{2,1,0:T(8,128)(2,1)}), bf16[8,512,128]{2,1,0:T(8,128)(2,1)S(1)}, u32[]{:S(2)}, u32[]{:S(2)}) async-start(bf16[8,512,128]{2,1,0:T(8,128)(2,1)} %broadcast_in_dim.79), calls=%async_computation.3 | async-start | bytes 2097152 | tf_op jit(solution)/shard_map/all_to_all | solution.py:28
  158.0 30.9 %collective-permute-start.4 = (bf16[256,128]{0,1:T(8,128)(2,1)}, bf16[256,128]{0,1:T(8,128)(2,1)}, u32[]{:S(2)}, u32[]{:S(2)}) collective-permute-start(bf16[256,128]{0,1:T(8,128)(2,1)} %fusion.1), channel_id=1, source_target_pairs={{0,32},{8,40},{16,48},{24,56},{32,64},{40,72},{48,80},{56,88},{64,... | collective-permute-start | bytes 196616 | tf_op jit(solution)/shard_map/ppermute | solution.py:24
  160.5 29.2 %collective-permute-start.5 = (bf16[256,128]{0,1:T(8,128)(2,1)}, bf16[256,128]{0,1:T(8,128)(2,1)}, u32[]{:S(2)}, u32[]{:S(2)}) collective-permute-start(bf16[256,128]{0,1:T(8,128)(2,1)} %fusion.1), channel_id=1, source_target_pairs={{0,24},{8,32},{16,40},{24,48},{32,56},{40,64},{48,72},{56,80},{64,... | collective-permute-start | bytes 196616 | tf_op jit(solution)/shard_map/ppermute | solution.py:24
  164.9 25.6 %collective-permute-start.6 = (bf16[256,128]{0,1:T(8,128)(2,1)}, bf16[256,128]{0,1:T(8,128)(2,1)}, u32[]{:S(2)}, u32[]{:S(2)}) collective-permute-start(bf16[256,128]{0,1:T(8,128)(2,1)} %fusion.1), channel_id=1, source_target_pairs={{0,16},{8,24},{16,32},{24,40},{32,48},{40,56},{48,64},{56,72},{64,... | collective-permute-start | bytes 196616 | tf_op jit(solution)/shard_map/ppermute | solution.py:24
  171.1 20.3 %collective-permute-start.7 = (bf16[256,128]{0,1:T(8,128)(2,1)}, bf16[256,128]{0,1:T(8,128)(2,1)}, u32[]{:S(2)}, u32[]{:S(2)}) collective-permute-start(bf16[256,128]{0,1:T(8,128)(2,1)} %fusion.1), channel_id=1, source_target_pairs={{0,8},{8,16},{16,24},{24,32},{32,40},{40,48},{48,56},{56,64},{64,7... | collective-permute-start | bytes 196616 | tf_op jit(solution)/shard_map/ppermute | solution.py:24
  173.4 46.6 %all-to-all-start.6 = ((bf16[8,64,128]{2,1,0:T(8,128)(2,1)}), bf16[8,64,128]{2,1,0:T(8,128)(2,1)}, u32[]{:S(2)}, u32[]{:S(2)}) async-start(bf16[8,64,128]{2,1,0:T(8,128)(2,1)} %bitcast.103), calls=%async_computation.6 | async-start | bytes 262144 | tf_op jit(solution)/shard_map/all_to_all | solution.py:28
  183.7 9.4 %copy-start.2 = (bf16[1024,1280]{1,0:T(8,128)(2,1)S(1)}, bf16[1024,1280]{1,0:T(8,128)(2,1)}, u32[]{:S(2)}) copy-start(bf16[1024,1280]{1,0:T(8,128)(2,1)} %copy-done.1) | copy-start | bytes 7864324
  183.7 9.4 %copy-start.13 = (bf16[256,1,128]{0,2,1:T(8,128)(2,1)S(1)}, bf16[256,1,128]{0,2,1:T(8,128)(2,1)}, u32[]{:S(2)}) copy-start(bf16[256,1,128]{0,2,1:T(8,128)(2,1)} %copy-done.12) | copy-start | bytes 196612
  183.7 9.4 %copy-start.15 = (bf16[256,1,128]{0,2,1:T(8,128)(2,1)S(1)}, bf16[256,1,128]{0,2,1:T(8,128)(2,1)}, u32[]{:S(2)}) copy-start(bf16[256,1,128]{0,2,1:T(8,128)(2,1)} %copy-done.14) | copy-start | bytes 196612
  183.7 9.4 %copy-start.17 = (bf16[256,1,128]{0,2,1:T(8,128)(2,1)S(1)}, bf16[256,1,128]{0,2,1:T(8,128)(2,1)}, u32[]{:S(2)}) copy-start(bf16[256,1,128]{0,2,1:T(8,128)(2,1)} %copy-done.16) | copy-start | bytes 196612
  183.7 9.4 %copy-start.19 = (bf16[256,1,128]{0,2,1:T(8,128)(2,1)S(1)}, bf16[256,1,128]{0,2,1:T(8,128)(2,1)}, u32[]{:S(2)}) copy-start(bf16[256,1,128]{0,2,1:T(8,128)(2,1)} %copy-done.18) | copy-start | bytes 196612
  197.8 23.7 %collective-permute-start.10 = (bf16[256,128]{1,0:T(8,128)(2,1)}, bf16[256,128]{1,0:T(8,128)(2,1)S(1)}, u32[]{:S(2)}, u32[]{:S(2)}) collective-permute-start(bf16[256,128]{1,0:T(8,128)(2,1)} %get-tuple-element.26), channel_id=1, source_target_pairs={{24,0},{32,8},{40,16},{48,24},{56,32},{64,40},{72,48},{80,56},{88,... | collective-permute-start | bytes 196616 | tf_op jit(solution)/shard_map/ppermute | solution.py:24
  206.9 14.7 %collective-permute-start.11 = (bf16[256,128]{1,0:T(8,128)(2,1)}, bf16[256,128]{1,0:T(8,128)(2,1)S(1)}, u32[]{:S(2)}, u32[]{:S(2)}) collective-permute-start(bf16[256,128]{1,0:T(8,128)(2,1)} %get-tuple-element.25), channel_id=1, source_target_pairs={{32,0},{40,8},{48,16},{56,24},{64,32},{72,40},{80,48},{88,56},{96,... | collective-permute-start | bytes 196616 | tf_op jit(solution)/shard_map/ppermute | solution.py:24
  210.3 11.3 %collective-permute-start.8 = (bf16[256,128]{1,0:T(8,128)(2,1)}, bf16[256,128]{1,0:T(8,128)(2,1)S(1)}, u32[]{:S(2)}, u32[]{:S(2)}) collective-permute-start(bf16[256,128]{1,0:T(8,128)(2,1)} %get-tuple-element.24), channel_id=1, source_target_pairs={{8,0},{16,8},{24,16},{32,24},{40,32},{48,40},{56,48},{64,56},{72,6... | collective-permute-start | bytes 196616 | tf_op jit(solution)/shard_map/ppermute | solution.py:24
  212.2 9.4 %collective-permute-start.9 = (bf16[256,128]{1,0:T(8,128)(2,1)}, bf16[256,128]{1,0:T(8,128)(2,1)S(1)}, u32[]{:S(2)}, u32[]{:S(2)}) collective-permute-start(bf16[256,128]{1,0:T(8,128)(2,1)} %get-tuple-element.27), channel_id=1, source_target_pairs={{16,0},{24,8},{32,16},{40,24},{48,32},{56,40},{64,48},{72,56},{80,... | collective-permute-start | bytes 196616 | tf_op jit(solution)/shard_map/ppermute | solution.py:24
  (10 other events, 47.5 us)

commit v2 on v1

v2 whole, which is shorter than its diff:
```python
import functools
import math

import jax
import jax.numpy as jnp
from jax import lax
from jax.experimental import pallas as pl
from jax.experimental.pallas import tpu as pltpu
from jax.sharding import PartitionSpec as P

SPAN = 4
Z = 8
YX = 8
F32 = jnp.float32
BF16 = jnp.bfloat16
NT = (((1,), (1,)), ((), ()))
NN = (((1,), (0,)), ((), ()))

Z_GROUPS = [[a * Z + z for z in range(Z)] for a in range(YX)]
YX_GROUPS = [[a * Z + z for a in range(YX)] for z in range(Z)]

tie = lax.optimization_barrier


def shifted(value, steps):
    count = lax.axis_size("dp")
    first, last = (max(0, -steps), min(count, count - steps))
    return lax.ppermute(value, "dp", [(source, source + steps) for source in range(first, last)])


def swap_all(value, groups):
    return lax.all_to_all(value, "dp", 0, 0, tiled=True, axis_index_groups=groups)


def copies(value, count):
    return jnp.broadcast_to(value[None], (count,) + value.shape).reshape(
        (count * value.shape[0],) + value.shape[1:]
    )


def mm(a, b, dims):
    return lax.dot_general(a, b, dims, preferred_element_type=F32)


def fill_window(win, own, h1, h2, h34):
    tok = own.shape[0]
    win[0:tok] = h34[tok:]
    win[tok : 2 * tok] = h34[:tok]
    win[2 * tok : 3 * tok] = h2[...]
    win[3 * tok : 4 * tok] = h1[...]
    win[4 * tok :] = own[...]


def masked_scores(factor, first, win, q_g, start):
    keys = win.shape[0]
    tok = q_g.shape[0]
    key_pos = first - SPAN * tok + lax.broadcasted_iota(jnp.int32, (keys, tok), 0)
    query_pos = first + lax.broadcasted_iota(jnp.int32, (keys, tok), 1)
    allowed = (key_pos >= start) & (key_pos <= query_pos)
    return jnp.where(allowed, mm(win, q_g, NT) * factor, -1e30)


def add_to(acc, part, first):
    if first:
        acc[...] = part
    else:
        acc[...] += part


def store_grads(acc, own, g12, g34):
    tok = own.shape[0]
    own[...] = acc[4 * tok :]
    g12[0:tok] = acc[3 * tok : 4 * tok]
    g12[tok:] = acc[2 * tok : 3 * tok]
    g34[0:tok] = acc[tok : 2 * tok].astype(BF16)
    g34[tok:] = acc[0:tok].astype(BF16)


def probs_kernel(
    factor, base, q, do, k0, k1, k2, k34, start, unused, lse, dv_own, dv12, dv34, kwin, acc
):
    width = k0.shape[1]
    fill_window(kwin, k0, k1, k2, k34)
    for g in range(q.shape[1] // width):
        cols = slice(g * width, (g + 1) * width)
        scores = masked_scores(factor, base[0], kwin[...], q[:, cols], start[...])
        top = jnp.max(scores, axis=0, keepdims=True)
        e = jnp.exp(scores - top)
        total = jnp.sum(e, axis=0, keepdims=True)
        lse[g : g + 1] = top + jnp.log(total)
        p = (e * (1.0 / total)).astype(BF16)
        add_to(acc, mm(p, do[:, cols], NN), g == 0)
    store_grads(acc, dv_own, dv12, dv34)


def attention_kernel(
    factor, base, q, do, k0, k1, k2, k34, v0, v1, v2, v34, start, lse,
    out, dq, dk_own, dk12, dk34, kwin, vwin, acc,
):
    width = k0.shape[1]
    fill_window(kwin, k0, k1, k2, k34)
    fill_window(vwin, v0, v1, v2, v34)
    k_cols = kwin[...].T
    v_cols = vwin[...].T
    for g in range(q.shape[1] // width):
        cols = slice(g * width, (g + 1) * width)
        do_g = do[:, cols]
        scores = masked_scores(factor, base[0], kwin[...], q[:, cols], start[...])
        p = jnp.exp(scores - lse[g : g + 1]).astype(BF16)
        attn = mm(v_cols, p, NN).astype(BF16).astype(F32)
        delta = jnp.sum(do_g.astype(F32).T * attn, axis=0, keepdims=True)
        out[:, cols] = attn.T.astype(BF16)
        dprob = mm(vwin[...], do_g, NT)
        ds = (p.astype(F32) * (dprob - delta) * factor).astype(BF16)
        dq[:, cols] = mm(k_cols, ds, NN).T.astype(BF16)
        add_to(acc, mm(ds, q[:, cols], NN), g == 0)
    store_grads(acc, dk_own, dk12, dk34)


def weight_copies_kernel(exponent, codes, out):
    e = exponent[0, 0]
    scale = jnp.float32(0.0)
    for level, power in zip(range(-2, 2), (0.25, 0.5, 1.0, 2.0)):
        scale = jnp.where(e == level, jnp.float32(power), scale)
    w = (codes[...].astype(F32) * scale).astype(BF16)
    for i in range(out.shape[0]):
        out[i] = w


def total_grad(own, r1, r2):
    return (own[...] + r1[...].astype(F32) + r2[...].astype(F32)).astype(BF16)


def input_grad_kernel(w, own, r1, r2, out):
    out[...] = mm(w[...], total_grad(own, r1, r2), NT).astype(BF16)


def weight_grad_kernel(x, own, r1, r2, out):
    out[...] = mm(x[...], total_grad(own, r1, r2), NN).astype(BF16)


def near_kernel(g12, r34, unused, near1, near2):
    tok = near1.shape[0]
    near1[...] = (g12[0:tok] + r34[0:tok].astype(F32)).astype(BF16)
    near2[...] = (g12[tok:] + r34[tok:].astype(F32)).astype(BF16)


def sum_kernel(parts, unused, out):
    total = parts[0].astype(F32)
    for i in range(1, parts.shape[0]):
        total += parts[i].astype(F32)
    out[...] = total.astype(out.dtype)


def body(x, codes, exponents, queries, keys, doc_start, cotangent):
    feat, tok = x.shape
    width = keys.shape[2]
    group = queries.shape[2] // width
    window = (SPAN + 1) * tok
    heads = lax.axis_size("tensor")
    factor = 1.0 / math.sqrt(width)
    base = (lax.axis_index("dp") * tok).astype(jnp.int32).reshape(1)
    vmem = pl.BlockSpec(memory_space=pltpu.VMEM)
    smem = pl.BlockSpec(memory_space=pltpu.SMEM)
    anywhere = pl.BlockSpec(memory_space=pl.ANY)
    params = pltpu.CompilerParams(vmem_limit_bytes=14 * 1024 * 1024)

    k0 = keys[:, 0, :]
    q = queries[:, 0, :]
    do = cotangent[:, 0, :]
    start = doc_start[None, :]

    w_copies = pl.pallas_call(
        weight_copies_kernel,
        out_shape=jax.ShapeDtypeStruct((Z, feat // (Z * YX), width), BF16),
        in_specs=[smem, vmem],
        out_specs=vmem,
        compiler_params=params,
    )(exponents, codes[:, 0, :])
    w_block = swap_all(w_copies.reshape(feat // YX, width), Z_GROUPS)

    k1 = shifted(k0, 1)
    k2 = shifted(k0, 2)
    w_full = swap_all(copies(w_block, YX), YX_GROUPS)
    k34 = shifted(jnp.concatenate([k1, k2], axis=0), 2)
    v0 = lax.dot_general(
        x, w_full, (((0,), (0,)), ((), ())), preferred_element_type=F32
    ).astype(BF16)
    v1 = shifted(v0, 1)
    v2 = shifted(v0, 2)

    grads_shape = [
        jax.ShapeDtypeStruct((tok, width), F32),
        jax.ShapeDtypeStruct((2 * tok, width), F32),
        jax.ShapeDtypeStruct((2 * tok, width), BF16),
    ]
    lse, dv_own, dv12, dv34 = pl.pallas_call(
        functools.partial(probs_kernel, factor),
        out_shape=[jax.ShapeDtypeStruct((group, tok), F32)] + grads_shape,
        in_specs=[smem] + [vmem] * 7 + [anywhere],
        out_specs=[vmem] * 4,
        scratch_shapes=[pltpu.VMEM((window, width), BF16), pltpu.VMEM((window, width), F32)],
        compiler_params=params,
    )(base, q, do, k0, k1, k2, k34, start, v0)


    def near_sum(g12, r34, unused):
        return pl.pallas_call(
            near_kernel,
            out_shape=[jax.ShapeDtypeStruct((tok, width), BF16)] * 2,
            in_specs=[vmem] * 2 + [anywhere],
            out_specs=[vmem] * 2,
            compiler_params=params,
        )(g12, r34, unused)

    r34 = shifted(dv34, -2)
    near1, near2 = near_sum(dv12, r34, v1)
    r1 = shifted(near1, -1)
    r2 = shifted(near2, -2)
    v34 = shifted(jnp.concatenate([v1, v2], axis=0), 2)

    r1, v34 = tie((r1, v34))

    blocks = heads
    same = pl.BlockSpec((tok, width), lambda i: (0, 0))
    d_part = pl.pallas_call(
        input_grad_kernel,
        grid=(blocks,),
        out_shape=jax.ShapeDtypeStruct((feat, tok), BF16),
        in_specs=[pl.BlockSpec((feat // blocks, width), lambda i: (i, 0)), same, same, same],
        out_specs=pl.BlockSpec((feat // blocks, tok), lambda i: (i, 0)),
        compiler_params=params,
    )(w_full, dv_own, r1, r2)
    d_input = lax.psum_scatter(d_part, "tensor", scatter_dimension=0, tiled=True)
    dw_part = pl.pallas_call(
        weight_grad_kernel,
        grid=(blocks,),
        out_shape=jax.ShapeDtypeStruct((feat, width), BF16),
        in_specs=[pl.BlockSpec((feat // blocks, tok), lambda i: (i, 0)), same, same, same],
        out_specs=pl.BlockSpec((feat // blocks, width), lambda i: (i, 0)),
        compiler_params=params,
    )(x, dv_own, r1, r2)

    dw_block = swap_all(dw_part, YX_GROUPS)
    out, dq, dk_own, dk12, dk34 = pl.pallas_call(
        functools.partial(attention_kernel, factor),
        out_shape=[jax.ShapeDtypeStruct((tok, group * width), BF16)] * 2 + grads_shape,
        in_specs=[smem] + [vmem] * 12,
        out_specs=[vmem] * 5,
        scratch_shapes=[
            pltpu.VMEM((window, width), BF16),
            pltpu.VMEM((window, width), BF16),
            pltpu.VMEM((window, width), F32),
        ],
        compiler_params=params,
    )(base, q, do, k0, k1, k2, k34, v0, v1, v2, v34, start, lse)
    dw_block = pl.pallas_call(
        sum_kernel,
        out_shape=jax.ShapeDtypeStruct((feat // YX, width), BF16),
        in_specs=[vmem, anywhere],
        out_specs=vmem,
        compiler_params=params,
    )(dw_block.reshape(YX, feat // YX, width), dk34)
    dw_own = swap_all(dw_block, Z_GROUPS)
    s1, s2 = near_sum(dk12, shifted(dk34, -2), dw_block)
    projection_gradient = pl.pallas_call(
        sum_kernel,
        out_shape=jax.ShapeDtypeStruct((feat // (YX * Z), width), F32),
        in_specs=[vmem, anywhere],
        out_specs=vmem,
        compiler_params=params,
    )(dw_own.reshape(Z, feat // (YX * Z), width), dk34)
    s1 = shifted(s1, -1)
    s2 = shifted(s2, -2)
    d_keys = (
        dk_own + s1.astype(F32) + s2.astype(F32)
    ).astype(BF16)
    return (
        out[:, None, :],
        dq[:, None, :],
        d_keys[:, None, :],
        d_input,
        projection_gradient[:, None, :],
    )


def solution(mesh):
    in_specs = (
        P(None, "dp"),
        P("dp", "tensor", None),
        P("dp", "tensor"),
        P("dp", "tensor", None),
        P("dp", "tensor", None),
        P("dp"),
        P("dp", "tensor", None),
    )
    out_specs = (
        P("dp", "tensor", None),
        P("dp", "tensor", None),
        P("dp", "tensor", None),
        P("tensor", "dp"),
        P("dp", "tensor", None),
    )
    return jax.shard_map(body, mesh=mesh, in_specs=in_specs, out_specs=out_specs, check_vma=False)
```

time: 226 us -> 162 us (0.72)
  the two profiles are of different devices: /device:TPU:56 before, /device:TPU:40 now
where the time goes in v2:
time: 162 us; the launch traced here: 161 us
  starting transfers between devices  60.4 us (37%)
  waiting for transfers between devices  35.9 us (22%)
  blocking collectives  19.2 us (12%)
  Pallas kernels  17.6 us (11%)
  between operations  15.1 us (9%)
  local copies, waits for them, and re-layouts  9.51 us (6%)
  other arithmetic  2.2 us (1%)
    ppermute x12, starting transfers between devices, shifted(): lax.ppermute(value, 'dp', [(source, source + steps) for source in range(f...  46.8 us
    ppermute x12, waiting for transfers between devices, shifted(): lax.ppermute(value, 'dp', [(source, source + steps) for source in range(f...  28.6 us
    all_to_all x1, blocking collectives, swap_all(): lax.all_to_all(value, 'dp', 0, 0, tiled=True, axis_index_groups=groups)  19.2 us
    all_to_all x3, starting transfers between devices, swap_all(): lax.all_to_all(value, 'dp', 0, 0, tiled=True, axis_index_groups=groups)  13.6 us
    unnamed x48, local copies, waits for them, and re-layouts  8.36 us
    all_to_all x3, waiting for transfers between devices, swap_all(): lax.all_to_all(value, 'dp', 0, 0, tiled=True, axis_index_groups=groups)  7.33 us
    pallas_call x1, Pallas kernels, body(): pl.pallas_call(functools.partial(attention_kernel, factor), out_shape=[ja...  6.61 us
    pallas_call x1, Pallas kernels, body(): pl.pallas_call(functools.partial(probs_kernel, factor), out_shape=[jax.Sh...  3.82 us
  transfers between devices with their start and end apart: 16, of which 7 were waited for; matrix products, arithmetic and copies ran while one was open for 2% of the time, Pallas kernels for 10%

profile of v2, /device:TPU:40, one launch (start us, length us, event | category | flops | bytes accessed | tf_op | source)
XLA Modules:
  0.0 160.9 jit_solution(7509020313586581166)
XLA Ops:
  8.7 19.2 %all_to_all.32 = bf16[8,64,128]{2,1,0:T(8,128)(2,1)S(1)} all-to-all(bf16[8,64,128]{2,1,0:T(8,128)(2,1)S(1)} %shard_map.110), channel_id=1, replica_groups={{0,8,16,24,32,40,48,56},{64,72,80,88,96,104,112,120},{128,136,144,152,1..., dimensions={0} | all-to-all | bytes 262144 | tf_op jit(solution)/shard_map/all_to_all | solution.py:32
  27.9 1.1 broadcast_in_dim.24
  29.1 5.8 %all-to-all-start.1 = ((bf16[8,512,128]{2,1,0:T(8,128)(2,1)}), bf16[8,512,128]{2,1,0:T(8,128)(2,1)S(1)}, u32[]{:S(2)}, u32[]{:S(2)}) async-start(bf16[8,512,128]{2,1,0:T(8,128)(2,1)} %broadcast_in_dim.24), calls=%async_computation.1 | async-start | bytes 2097152 | tf_op jit(solution)/shard_map/all_to_all | solution.py:32
  34.9 2.1 %collective-permute-start.1 = (bf16[256,128]{1,0:T(8,128)(2,1)S(1)}, bf16[256,128]{1,0:T(8,128)(2,1)S(1)}, u32[]{:S(2)}, u32[]{:S(2)}) collective-permute-start(bf16[256,128]{1,0:T(8,128)(2,1)S(1)} %bitcast.27), channel_id=1, source_target_pairs={{0,16},{8,24},{16,32},{24,40},{32,48},{40,56},{48,64},{56,72},{64,... | collective-permute-start | bytes 196616 | tf_op jit(solution)/shard_map/ppermute | solution.py:28
  37.0 3.0 %collective-permute-start = (bf16[256,128]{1,0:T(8,128)(2,1)S(1)}, bf16[256,128]{1,0:T(8,128)(2,1)S(1)}, u32[]{:S(2)}, u32[]{:S(2)}) collective-permute-start(bf16[256,128]{1,0:T(8,128)(2,1)S(1)} %bitcast.28), channel_id=1, source_target_pairs={{0,8},{8,16},{16,24},{24,32},{32,40},{40,48},{48,56},{56,64},{64,7... | collective-permute-start | bytes 196616 | tf_op jit(solution)/shard_map/ppermute | solution.py:28
  40.0 10.6 %collective-permute-done.1.k2 = bf16[256,128]{1,0:T(8,128)(2,1)S(1)} collective-permute-done((bf16[256,128]{1,0:T(8,128)(2,1)S(1)}, bf16[256,128]{1,0:T(8,128)(2,1)S(1)}, u32[]{:S(2)}, u32[]{:S(2)}) %collective-permute-start.1) | collective-permute-done | bytes 65568 | tf_op jit(solution)/shard_map/ppermute | solution.py:28
  51.3 1.9 %collective-permute-start.2 = (bf16[512,128]{1,0:T(8,128)(2,1)}, bf16[512,128]{1,0:T(8,128)(2,1)}, u32[]{:S(2)}, u32[]{:S(2)}) collective-permute-start(bf16[512,128]{1,0:T(8,128)(2,1)} %pad_maximum_fusion), channel_id=1, source_target_pairs={{0,16},{8,24},{16,32},{24,40},{32,48},{40,56},{48,64},{56,72},{64,... | collective-permute-start | bytes 393224 | tf_op jit(solution)/shard_map/ppermute | solution.py:28
  53.2 0.9 fusion.unused.v0
  54.2 1.9 %collective-permute-start.4 = (bf16[256,128]{1,0:T(8,128)(2,1)S(1)}, bf16[256,128]{1,0:T(8,128)(2,1)}, u32[]{:S(2)}, u32[]{:S(2)}) collective-permute-start(bf16[256,128]{1,0:T(8,128)(2,1)S(1)} %fusion.unused.v0), channel_id=1, source_target_pairs={{0,16},{8,24},{16,32},{24,40},{32,48},{40,56},{48,64},{56,72},{64,... | collective-permute-start | bytes 196616 | tf_op jit(solution)/shard_map/ppermute | solution.py:28
  56.1 2.0 %collective-permute-start.3 = (bf16[256,128]{1,0:T(8,128)(2,1)S(1)}, bf16[256,128]{1,0:T(8,128)(2,1)S(1)}, u32[]{:S(2)}, u32[]{:S(2)}) collective-permute-start(bf16[256,128]{1,0:T(8,128)(2,1)S(1)} %fusion.unused.v0), channel_id=1, source_target_pairs={{0,8},{8,16},{16,24},{24,32},{32,40},{40,48},{48,56},{56,64},{64,7... | collective-permute-start | bytes 196616 | tf_op jit(solution)/shard_map/ppermute | solution.py:28
  58.1 7.2 %collective-permute-done.2.k34 = bf16[512,128]{1,0:T(8,128)(2,1)} collective-permute-done((bf16[512,128]{1,0:T(8,128)(2,1)}, bf16[512,128]{1,0:T(8,128)(2,1)}, u32[]{:S(2)}, u32[]{:S(2)}) %collective-permute-start.2) | collective-permute-done | bytes 131104 | tf_op jit(solution)/shard_map/ppermute | solution.py:28
  65.3 0.9 copy-done.3
  68.7 3.8 %shard_map.111 = (f32[4,256]{1,0:T(4,128)S(1)}, f32[256,128]{1,0:T(8,128)S(1)}, f32[512,128]{1,0:T(8,128)S(1)}, bf16[512,128]{1,0:T(8,128)(2,1)S(1)}) custom-call(s32[1]{0:T(128)} %bitcast.base, bf16[256,512]{1,0:T(8,128)(2,1)S(1)} %bitcast.23, bf16[256,512]{1,0:T(8,128)(2,1)S(1)} %bitcast.25, bf16[256,128]{1,0:T(8,128)(2,1)S(1)} %bitcast.29, ...), custom_call_target="tpu_custom_call" | custom-call | tf_op jit(solution)/shard_map/pallas_call | solution.py:197
  72.6 1.9 %collective-permute-start.5 = (bf16[512,128]{1,0:T(8,128)(2,1)S(1)}, bf16[512,128]{1,0:T(8,128)(2,1)S(1)}, u32[]{:S(2)}, u32[]{:S(2)}) collective-permute-start(bf16[512,128]{1,0:T(8,128)(2,1)S(1)} %get-tuple-element.21), channel_id=1, source_target_pairs={{16,0},{24,8},{32,16},{40,24},{48,32},{56,40},{64,48},{72,56},{80,... | collective-permute-start | bytes 393224 | tf_op jit(solution)/shard_map/ppermute | solution.py:28
  75.4 4.8 %collective-permute-start.7 = (bf16[512,128]{1,0:T(8,128)(2,1)S(1)}, bf16[512,128]{1,0:T(8,128)(2,1)S(1)}, u32[]{:S(2)}, u32[]{:S(2)}) collective-permute-start(bf16[512,128]{1,0:T(8,128)(2,1)S(1)} %pad_maximum_fusion.1), channel_id=1, source_target_pairs={{0,16},{8,24},{16,32},{24,40},{32,48},{40,56},{48,64},{56,72},{64,... | collective-permute-start | bytes 393224 | tf_op jit(solution)/shard_map/ppermute | solution.py:28
  80.2 1.3 collective-permute-done.5.r34
  81.5 5.2 %collective-permute-start.6 = (bf16[256,128]{1,0:T(8,128)(2,1)S(1)}, bf16[256,128]{1,0:T(8,128)(2,1)S(1)}, u32[]{:S(2)}, u32[]{:S(2)}) collective-permute-start(bf16[256,128]{1,0:T(8,128)(2,1)S(1)} %get-tuple-element.22), channel_id=1, source_target_pairs={{8,0},{16,8},{24,16},{32,24},{40,32},{48,40},{56,48},{64,56},{72,6... | collective-permute-start | bytes 196616 | tf_op jit(solution)/shard_map/ppermute | solution.py:28
  86.8 3.1 %collective-permute-start.9 = (bf16[256,128]{1,0:T(8,128)(2,1)S(1)}, bf16[256,128]{1,0:T(8,128)(2,1)S(1)}, u32[]{:S(2)}, u32[]{:S(2)}) collective-permute-start(bf16[256,128]{1,0:T(8,128)(2,1)S(1)} %get-tuple-element.32), channel_id=1, source_target_pairs={{16,0},{24,8},{32,16},{40,24},{48,32},{56,40},{64,48},{72,56},{80,... | collective-permute-start | bytes 196616 | tf_op jit(solution)/shard_map/ppermute | solution.py:28
  90.5 3.3 %collective-permute-done.9.r2 = bf16[256,128]{1,0:T(8,128)(2,1)S(1)} collective-permute-done((bf16[256,128]{1,0:T(8,128)(2,1)S(1)}, bf16[256,128]{1,0:T(8,128)(2,1)S(1)}, u32[]{:S(2)}, u32[]{:S(2)}) %collective-permute-start.9) | collective-permute-done | bytes 65568 | tf_op jit(solution)/shard_map/ppermute | solution.py:28
  93.8 1.9 %shard_map.117 = bf16[4096,256]{1,0:T(8,128)(2,1)S(1)} custom-call(bf16[4096,128]{1,0:T(8,128)(2,1)S(1)} %bitcast.22, f32[256,128]{1,0:T(8,128)S(1)} %get-tuple-element.30.own, bf16[256,128]{1,0:T(8,128)(2,1)S(1)} %collective-permute-done.6.r1, bf16[256,128]{1,0:T(8,128)(2,1)S(1)} %collective-permute-done.9.r2), custom_call_target="tpu_custom_call" | custom-call | tf_op jit(solution)/shard_map/pallas_call | solution.py:226
  95.7 1.3 copy-done.1
  98.3 0.9 copy-done.12
  99.2 3.8 %shard_map.114 = bf16[4096,128]{1,0:T(8,128)(2,1)} custom-call(bf16[4096,256]{1,0:T(8,128)(2,1)S(1)} %copy-done, f32[256,128]{1,0:T(8,128)S(1)} %copy-done.12, bf16[256,128]{1,0:T(8,128)(2,1)S(1)} %copy-done.17, bf16[256,128]{1,0:T(8,128)(2,1)S(1)} %copy-done.19), custom_call_target="tpu_custom_call" | custom-call | tf_op jit(solution)/shard_map/pallas_call | solution.py:235
  103.0 3.6 %all-to-all-start.2 = ((bf16[8,512,128]{2,1,0:T(8,128)(2,1)}), bf16[8,512,128]{2,1,0:T(8,128)(2,1)S(1)}, u32[]{:S(2)}, u32[]{:S(2)}) async-start(bf16[8,512,128]{2,1,0:T(8,128)(2,1)} %bitcast.11), calls=%async_computation.2 | async-start | bytes 2097152 | tf_op jit(solution)/shard_map/all_to_all | solution.py:32
  106.7 6.6 %shard_map.113 = (bf16[256,512]{1,0:T(8,128)(2,1)}, bf16[256,512]{1,0:T(8,128)(2,1)}, f32[256,128]{1,0:T(8,128)S(1)}, f32[512,128]{1,0:T(8,128)S(1)}, bf16[512,128]{1,0:T(8,128)(2,1)S(1)}) custom-call(s32[1]{0:T(128)} %bitcast.base, bf16[256,512]{1,0:T(8,128)(2,1)S(1)} %bitcast.24, bf16[256,512]{1,0:T(8,128)(2,1)S(1)} %bitcast.26, ...), custom_call_target="tpu_custom_call" | custom-call | tf_op jit(solution)/shard_map/pallas_call | solution.py:245
  113.3 8.3 %collective-permute-start.8 = (bf16[512,128]{1,0:T(8,128)(2,1)S(1)}, bf16[512,128]{1,0:T(8,128)(2,1)S(1)}, u32[]{:S(2)}, u32[]{:S(2)}) collective-permute-start(bf16[512,128]{1,0:T(8,128)(2,1)S(1)} %get-tuple-element.29.unused), channel_id=1, source_target_pairs={{16,0},{24,8},{32,16},{40,24},{48,32},{56,40},{64,48},{72,56},{80,... | collective-permute-start | bytes 393224 | tf_op jit(solution)/shard_map/ppermute | solution.py:28
  122.4 5.1 %collective-permute-done.8.r34 = bf16[512,128]{1,0:T(8,128)(2,1)S(1)} collective-permute-done((bf16[512,128]{1,0:T(8,128)(2,1)S(1)}, bf16[512,128]{1,0:T(8,128)(2,1)S(1)}, u32[]{:S(2)}, u32[]{:S(2)}) %collective-permute-start.8) | collective-permute-done | bytes 131104 | tf_op jit(solution)/shard_map/ppermute | solution.py:28
  127.6 10.6 %collective-permute-start.10 = (bf16[256,128]{1,0:T(8,128)(2,1)S(1)}, bf16[256,128]{1,0:T(8,128)(2,1)S(1)}, u32[]{:S(2)}, u32[]{:S(2)}) collective-permute-start(bf16[256,128]{1,0:T(8,128)(2,1)S(1)} %get-tuple-element.33), channel_id=1, source_target_pairs={{8,0},{16,8},{24,16},{32,24},{40,32},{48,40},{56,48},{64,56},{72,6... | collective-permute-start | bytes 196616 | tf_op jit(solution)/shard_map/ppermute | solution.py:28
  138.2 1.9 %collective-permute-start.11 = (bf16[256,128]{1,0:T(8,128)(2,1)S(1)}, bf16[256,128]{1,0:T(8,128)(2,1)S(1)}, u32[]{:S(2)}, u32[]{:S(2)}) collective-permute-start(bf16[256,128]{1,0:T(8,128)(2,1)S(1)} %get-tuple-element.34), channel_id=1, source_target_pairs={{16,0},{24,8},{32,16},{40,24},{48,32},{56,40},{64,48},{72,56},{80,... | collective-permute-start | bytes 196616 | tf_op jit(solution)/shard_map/ppermute | solution.py:28
  140.2 4.2 %all-to-all-start.3 = ((bf16[8,64,128]{2,1,0:T(8,128)(2,1)}), bf16[8,64,128]{2,1,0:T(8,128)(2,1)S(1)}, u32[]{:S(2)}, u32[]{:S(2)}) async-start(bf16[8,64,128]{2,1,0:T(8,128)(2,1)} %bitcast.13), calls=%async_computation.4 | async-start | bytes 262144 | tf_op jit(solution)/shard_map/all_to_all | solution.py:32
  144.4 1.1 collective-permute-done.11
  146.1 7.3 %all-to-all-done.3.parts = bf16[8,64,128]{2,1,0:T(8,128)(2,1)S(1)} async-done(((bf16[8,64,128]{2,1,0:T(8,128)(2,1)}), bf16[8,64,128]{2,1,0:T(8,128)(2,1)S(1)}, u32[]{:S(2)}, u32[]{:S(2)}) %all-to-all-start.3) | async-done | bytes 131104 | tf_op jit(solution)/shard_map/all_to_all | solution.py:32
  (64 shorter events, 9.0 us)
Async XLA Ops:
  7.2 27.7 %copy-start.13 = (bf16[256,1,128]{2,0,1:T(8,128)(2,1)S(1)}, bf16[256,1,128]{2,0,1:T(8,128)(2,1)}, u32[]{:S(2)}) copy-start(bf16[256,1,128]{2,0,1:T(8,128)(2,1)} %param.11) | copy-start | bytes 196612
  7.2 46.0 %copy-start = (bf16[4096,256]{1,0:T(8,128)(2,1)S(1)}, bf16[4096,256]{1,0:T(8,128)(2,1)}, u32[]{:S(2)}) copy-start(bf16[4096,256]{1,0:T(8,128)(2,1)} %x.1) | copy-start | bytes 6291460
  29.1 24.1 %all-to-all-start.1 = ((bf16[8,512,128]{2,1,0:T(8,128)(2,1)}), bf16[8,512,128]{2,1,0:T(8,128)(2,1)S(1)}, u32[]{:S(2)}, u32[]{:S(2)}) async-start(bf16[8,512,128]{2,1,0:T(8,128)(2,1)} %broadcast_in_dim.24), calls=%async_computation.1 | async-start | bytes 2097152 | tf_op jit(solution)/shard_map/all_to_all | solution.py:32
  34.8 30.4 %copy-start.2 = (bf16[256,1,512]{2,0,1:T(8,128)(2,1)S(1)}, bf16[256,1,512]{2,0,1:T(8,128)(2,1)}, u32[]{:S(2)}) copy-start(bf16[256,1,512]{2,0,1:T(8,128)(2,1)} %param.10) | copy-start | bytes 786436
  34.8 30.4 %copy-start.23 = (s32[256]{0:T(256)S(1)}, s32[256]{0:T(256)}, u32[]{:S(2)}) copy-start(s32[256]{0:T(256)} %param.12) | copy-start | bytes 3076
  34.8 119.3 %reduce-scatter.2.cloned.1.call-start = ((), (), s32[]{:S(2)}) async-start(), calls=%async_computation.5 | async-start | bytes 2359296 | tf_op jit(solution)/shard_map/reduce_scatter | solution.py:234
  34.9 15.7 %collective-permute-start.1 = (bf16[256,128]{1,0:T(8,128)(2,1)S(1)}, bf16[256,128]{1,0:T(8,128)(2,1)S(1)}, u32[]{:S(2)}, u32[]{:S(2)}) collective-permute-start(bf16[256,128]{1,0:T(8,128)(2,1)S(1)} %bitcast.27), channel_id=1, source_target_pairs={{0,16},{8,24},{16,32},{24,40},{32,48},{40,56},{48,64},{56,72},{64,... | collective-permute-start | bytes 196616 | tf_op jit(solution)/shard_map/ppermute | solution.py:28
  37.0 13.6 %collective-permute-start = (bf16[256,128]{1,0:T(8,128)(2,1)S(1)}, bf16[256,128]{1,0:T(8,128)(2,1)S(1)}, u32[]{:S(2)}, u32[]{:S(2)}) collective-permute-start(bf16[256,128]{1,0:T(8,128)(2,1)S(1)} %bitcast.28), channel_id=1, source_target_pairs={{0,8},{8,16},{16,24},{24,32},{32,40},{40,48},{48,56},{56,64},{64,7... | collective-permute-start | bytes 196616 | tf_op jit(solution)/shard_map/ppermute | solution.py:28
  51.3 14.0 %collective-permute-start.2 = (bf16[512,128]{1,0:T(8,128)(2,1)}, bf16[512,128]{1,0:T(8,128)(2,1)}, u32[]{:S(2)}, u32[]{:S(2)}) collective-permute-start(bf16[512,128]{1,0:T(8,128)(2,1)} %pad_maximum_fusion), channel_id=1, source_target_pairs={{0,16},{8,24},{16,32},{24,40},{32,48},{40,56},{48,64},{56,72},{64,... | collective-permute-start | bytes 393224 | tf_op jit(solution)/shard_map/ppermute | solution.py:28
  54.2 20.3 %collective-permute-start.4 = (bf16[256,128]{1,0:T(8,128)(2,1)S(1)}, bf16[256,128]{1,0:T(8,128)(2,1)}, u32[]{:S(2)}, u32[]{:S(2)}) collective-permute-start(bf16[256,128]{1,0:T(8,128)(2,1)S(1)} %fusion.unused.v0), channel_id=1, source_target_pairs={{0,16},{8,24},{16,32},{24,40},{32,48},{40,56},{48,64},{56,72},{64,... | collective-permute-start | bytes 196616 | tf_op jit(solution)/shard_map/ppermute | solution.py:28
  56.1 18.4 %collective-permute-start.3 = (bf16[256,128]{1,0:T(8,128)(2,1)S(1)}, bf16[256,128]{1,0:T(8,128)(2,1)S(1)}, u32[]{:S(2)}, u32[]{:S(2)}) collective-permute-start(bf16[256,128]{1,0:T(8,128)(2,1)S(1)} %fusion.unused.v0), channel_id=1, source_target_pairs={{0,8},{8,16},{16,24},{24,32},{32,40},{40,48},{48,56},{56,64},{64,7... | collective-permute-start | bytes 196616 | tf_op jit(solution)/shard_map/ppermute | solution.py:28
  65.3 1.0 copy-start.3
  66.2 0.8 copy-start.6
  72.6 21.3 %copy-start.11 = (f32[256,128]{1,0:T(8,128)}, f32[256,128]{1,0:T(8,128)S(1)}, u32[]{:S(2)}) copy-start(f32[256,128]{1,0:T(8,128)S(1)} %get-tuple-element.30.own) | copy-start | bytes 393220
  72.6 8.9 %collective-permute-start.5 = (bf16[512,128]{1,0:T(8,128)(2,1)S(1)}, bf16[512,128]{1,0:T(8,128)(2,1)S(1)}, u32[]{:S(2)}, u32[]{:S(2)}) collective-permute-start(bf16[512,128]{1,0:T(8,128)(2,1)S(1)} %get-tuple-element.21), channel_id=1, source_target_pairs={{16,0},{24,8},{32,16},{40,24},{48,32},{56,40},{64,48},{72,56},{80,... | collective-permute-start | bytes 393224 | tf_op jit(solution)/shard_map/ppermute | solution.py:28
  75.4 14.5 %collective-permute-start.7 = (bf16[512,128]{1,0:T(8,128)(2,1)S(1)}, bf16[512,128]{1,0:T(8,128)(2,1)S(1)}, u32[]{:S(2)}, u32[]{:S(2)}) collective-permute-start(bf16[512,128]{1,0:T(8,128)(2,1)S(1)} %pad_maximum_fusion.1), channel_id=1, source_target_pairs={{0,16},{8,24},{16,32},{24,40},{32,48},{40,56},{48,64},{56,72},{64,... | collective-permute-start | bytes 393224 | tf_op jit(solution)/shard_map/ppermute | solution.py:28
  81.5 9.0 %collective-permute-start.6 = (bf16[256,128]{1,0:T(8,128)(2,1)S(1)}, bf16[256,128]{1,0:T(8,128)(2,1)S(1)}, u32[]{:S(2)}, u32[]{:S(2)}) collective-permute-start(bf16[256,128]{1,0:T(8,128)(2,1)S(1)} %get-tuple-element.22), channel_id=1, source_target_pairs={{8,0},{16,8},{24,16},{32,24},{40,32},{48,40},{56,48},{64,56},{72,6... | collective-permute-start | bytes 196616 | tf_op jit(solution)/shard_map/ppermute | solution.py:28
  86.8 7.1 %collective-permute-start.9 = (bf16[256,128]{1,0:T(8,128)(2,1)S(1)}, bf16[256,128]{1,0:T(8,128)(2,1)S(1)}, u32[]{:S(2)}, u32[]{:S(2)}) collective-permute-start(bf16[256,128]{1,0:T(8,128)(2,1)S(1)} %get-tuple-element.32), channel_id=1, source_target_pairs={{16,0},{24,8},{32,16},{40,24},{48,32},{56,40},{64,48},{72,56},{80,... | collective-permute-start | bytes 196616 | tf_op jit(solution)/shard_map/ppermute | solution.py:28
  95.7 1.3 copy-start.1
  98.3 0.9 copy-start.12
  98.3 0.9 copy-start.17
  98.3 0.9 copy-start.19
  99.2 7.5 %copy-start.4 = (bf16[256,1,512]{2,0,1:T(8,128)(2,1)S(1)}, bf16[256,1,512]{2,0,1:T(8,128)(2,1)}, u32[]{:S(2)}) copy-start(bf16[256,1,512]{2,0,1:T(8,128)(2,1)} %param.13) | copy-start | bytes 786436
  99.2 7.5 %copy-start.7 = (bf16[256,128]{1,0:T(8,128)(2,1)S(1)}, bf16[256,128]{1,0:T(8,128)(2,1)}, u32[]{:S(2)}) copy-start(bf16[256,128]{1,0:T(8,128)(2,1)} %copy-done.5) | copy-start | bytes 196612
  99.2 7.5 %copy-start.10 = (bf16[256,128]{1,0:T(8,128)(2,1)S(1)}, bf16[256,128]{1,0:T(8,128)(2,1)}, u32[]{:S(2)}) copy-start(bf16[256,128]{1,0:T(8,128)(2,1)} %copy-done.8) | copy-start | bytes 196612
  99.2 7.5 %copy-start.15 = (bf16[256,1,128]{2,0,1:T(8,128)(2,1)S(1)}, bf16[256,1,128]{2,0,1:T(8,128)(2,1)}, u32[]{:S(2)}) copy-start(bf16[256,1,128]{2,0,1:T(8,128)(2,1)} %param.11) | copy-start | bytes 196612
  103.0 3.7 %copy-start.21 = (bf16[512,128]{1,0:T(8,128)(2,1)S(1)}, bf16[512,128]{1,0:T(8,128)(2,1)}, u32[]{:S(2)}) copy-start(bf16[512,128]{1,0:T(8,128)(2,1)} %copy-done.20) | copy-start | bytes 393220
  103.0 18.6 %all-to-all-start.2 = ((bf16[8,512,128]{2,1,0:T(8,128)(2,1)}), bf16[8,512,128]{2,1,0:T(8,128)(2,1)S(1)}, u32[]{:S(2)}, u32[]{:S(2)}) async-start(bf16[8,512,128]{2,1,0:T(8,128)(2,1)} %bitcast.11), calls=%async_computation.2 | async-start | bytes 2097152 | tf_op jit(solution)/shard_map/all_to_all | solution.py:32
  113.3 14.2 %collective-permute-start.8 = (bf16[512,128]{1,0:T(8,128)(2,1)S(1)}, bf16[512,128]{1,0:T(8,128)(2,1)S(1)}, u32[]{:S(2)}, u32[]{:S(2)}) collective-permute-start(bf16[512,128]{1,0:T(8,128)(2,1)S(1)} %get-tuple-element.29.unused), channel_id=1, source_target_pairs={{16,0},{24,8},{32,16},{40,24},{48,32},{56,40},{64,48},{72,56},{80,... | collective-permute-start | bytes 393224 | tf_op jit(solution)/shard_map/ppermute | solution.py:28
  127.6 16.8 %collective-permute-start.10 = (bf16[256,128]{1,0:T(8,128)(2,1)S(1)}, bf16[256,128]{1,0:T(8,128)(2,1)S(1)}, u32[]{:S(2)}, u32[]{:S(2)}) collective-permute-start(bf16[256,128]{1,0:T(8,128)(2,1)S(1)} %get-tuple-element.33), channel_id=1, source_target_pairs={{8,0},{16,8},{24,16},{32,24},{40,32},{48,40},{56,48},{64,56},{72,6... | collective-permute-start | bytes 196616 | tf_op jit(solution)/shard_map/ppermute | solution.py:28
  138.2 7.2 %collective-permute-start.11 = (bf16[256,128]{1,0:T(8,128)(2,1)S(1)}, bf16[256,128]{1,0:T(8,128)(2,1)S(1)}, u32[]{:S(2)}, u32[]{:S(2)}) collective-permute-start(bf16[256,128]{1,0:T(8,128)(2,1)S(1)} %get-tuple-element.34), channel_id=1, source_target_pairs={{16,0},{24,8},{32,16},{40,24},{48,32},{56,40},{64,48},{72,56},{80,... | collective-permute-start | bytes 196616 | tf_op jit(solution)/shard_map/ppermute | solution.py:28
  140.2 13.3 %all-to-all-start.3 = ((bf16[8,64,128]{2,1,0:T(8,128)(2,1)}), bf16[8,64,128]{2,1,0:T(8,128)(2,1)S(1)}, u32[]{:S(2)}, u32[]{:S(2)}) async-start(bf16[8,64,128]{2,1,0:T(8,128)(2,1)} %bitcast.13), calls=%async_computation.4 | async-start | bytes 262144 | tf_op jit(solution)/shard_map/all_to_all | solution.py:32
  (8 other events, 5.7 us)
Sparse Core Ops, SparseCore 0:
  98.4 45.5 reduce-scatter.1

commit v3 on v2

--- a/solution.py
+++ b/solution.py
@@ -42,13 +42,23 @@
     return lax.dot_general(a, b, dims, preferred_element_type=F32)
 
 
-def fill_window(win, own, h1, h2, h34):
+def window_parts(win, own, h1, h2, h34):
     tok = own.shape[0]
-    win[0:tok] = h34[tok:]
-    win[tok : 2 * tok] = h34[:tok]
-    win[2 * tok : 3 * tok] = h2[...]
-    win[3 * tok : 4 * tok] = h1[...]
-    win[4 * tok :] = own[...]
+    return [
+        (own, win.at[4 * tok : 5 * tok]),
+        (h1, win.at[3 * tok : 4 * tok]),
+        (h2, win.at[2 * tok : 3 * tok]),
+        (h34.at[0:tok], win.at[tok : 2 * tok]),
+        (h34.at[tok : 2 * tok], win.at[0:tok]),
+    ]
+
+
+def fetch(parts, sems):
+    moves = [pltpu.make_async_copy(a, b, sems.at[i]) for i, (a, b) in enumerate(parts)]
+    for move in moves:
+        move.start()
+    for move in moves:
+        move.wait()
 
 
 def masked_scores(factor, first, win, q_g, start):
@@ -77,10 +87,11 @@
 
 
 def probs_kernel(
-    factor, base, q, do, k0, k1, k2, k34, start, unused, lse, dv_own, dv12, dv34, kwin, acc
+    factor, base, q_in, do_in, k0, k1, k2, k34, start, unused, lse, dv_own, dv12, dv34,
+    q, do, kwin, acc, sems,
 ):
     width = k0.shape[1]
-    fill_window(kwin, k0, k1, k2, k34)
+    fetch([(q_in, q), (do_in, do)] + window_parts(kwin, k0, k1, k2, k34), sems)
     for g in range(q.shape[1] // width):
         cols = slice(g * width, (g + 1) * width)
         scores = masked_scores(factor, base[0], kwin[...], q[:, cols], start[...])
@@ -94,12 +105,16 @@
 
 
 def attention_kernel(
-    factor, base, q, do, k0, k1, k2, k34, v0, v1, v2, v34, start, lse,
-    out, dq, dk_own, dk12, dk34, kwin, vwin, acc,
+    factor, base, q_in, do_in, k0, k1, k2, k34, v0, v1, v2, v34, start, lse,
+    out, dq, dk_own, dk12, dk34, q, do, kwin, vwin, acc, sems,
 ):
     width = k0.shape[1]
-    fill_window(kwin, k0, k1, k2, k34)
-    fill_window(vwin, v0, v1, v2, v34)
+    fetch(
+        [(q_in, q), (do_in, do)]
+        + window_parts(kwin, k0, k1, k2, k34)
+        + window_parts(vwin, v0, v1, v2, v34),
+        sems,
+    )
     k_cols = kwin[...].T
     v_cols = vwin[...].T
     for g in range(q.shape[1] // width):
@@ -127,22 +142,20 @@
         out[i] = w
 
 
-def total_grad(own, r1, r2):
-    return (own[...] + r1[...].astype(F32) + r2[...].astype(F32)).astype(BF16)
-
-
-def input_grad_kernel(w, own, r1, r2, out):
-    out[...] = mm(w[...], total_grad(own, r1, r2), NT).astype(BF16)
-
-
-def weight_grad_kernel(x, own, r1, r2, out):
-    out[...] = mm(x[...], total_grad(own, r1, r2), NN).astype(BF16)
+def value_grad_kernel(x, w, own, r1, r2, d_in, d_w):
+    total = (own[...] + r1[...].astype(F32) + r2[...].astype(F32)).astype(BF16)
+    d_in[...] = mm(w[...], total, NT).astype(BF16)
+    d_w[...] = mm(x[...], total, NN).astype(BF16)
 
 
 def near_kernel(g12, r34, unused, near1, near2):
     tok = near1.shape[0]
     near1[...] = (g12[0:tok] + r34[0:tok].astype(F32)).astype(BF16)
     near2[...] = (g12[tok:] + r34[tok:].astype(F32)).astype(BF16)
+
+
+def total_kernel(own, r1, r2, unused, out):
+    out[...] = (own[...] + r1[...].astype(F32) + r2[...].astype(F32)).astype(BF16)
 
 
 def sum_kernel(parts, unused, out):
@@ -163,6 +176,7 @@
     vmem = pl.BlockSpec(memory_space=pltpu.VMEM)
     smem = pl.BlockSpec(memory_space=pltpu.SMEM)
     anywhere = pl.BlockSpec(memory_space=pl.ANY)
+    hbm = pl.BlockSpec(memory_space=pltpu.HBM)
     params = pltpu.CompilerParams(vmem_limit_bytes=14 * 1024 * 1024)
 
     k0 = keys[:, 0, :]
@@ -197,9 +211,15 @@
     lse, dv_own, dv12, dv34 = pl.pallas_call(
         functools.partial(probs_kernel, factor),
         out_shape=[jax.ShapeDtypeStruct((group, tok), F32)] + grads_shape,
-        in_specs=[smem] + [vmem] * 7 + [anywhere],
+        in_specs=[smem] + [hbm] * 6 + [vmem, anywhere],
         out_specs=[vmem] * 4,
-        scratch_shapes=[pltpu.VMEM((window, width), BF16), pltpu.VMEM((window, width), F32)],
+        scratch_shapes=[
+            pltpu.VMEM((tok, group * width), BF16),
+            pltpu.VMEM((tok, group * width), BF16),
+            pltpu.VMEM((window, width), BF16),
+            pltpu.VMEM((window, width), F32),
+            pltpu.SemaphoreType.DMA((7,)),
+        ],
         compiler_params=params,
     )(base, q, do, k0, k1, k2, k34, start, v0)
 
@@ -221,36 +241,36 @@
 
     r1, v34 = tie((r1, v34))
 
-    blocks = heads
+    blocks = 4
     same = pl.BlockSpec((tok, width), lambda i: (0, 0))
-    d_part = pl.pallas_call(
-        input_grad_kernel,
+    wide = pl.BlockSpec((feat // blocks, tok), lambda i: (i, 0))
+    narrow = pl.BlockSpec((feat // blocks, width), lambda i: (i, 0))
+    d_part, dw_part = pl.pallas_call(
+        value_grad_kernel,
         grid=(blocks,),
-        out_shape=jax.ShapeDtypeStruct((feat, tok), BF16),
-        in_specs=[pl.BlockSpec((feat // blocks, width), lambda i: (i, 0)), same, same, same],
-        out_specs=pl.BlockSpec((feat // blocks, tok), lambda i: (i, 0)),
-        compiler_params=params,
-    )(w_full, dv_own, r1, r2)
+        out_shape=[
+            jax.ShapeDtypeStruct((feat, tok), BF16),
+            jax.ShapeDtypeStruct((feat, width), BF16),
+        ],
+        in_specs=[wide, narrow, same, same, same],
+        out_specs=[wide, narrow],
+        compiler_params=params,
+    )(x, w_full, dv_own, r1, r2)
     d_input = lax.psum_scatter(d_part, "tensor", scatter_dimension=0, tiled=True)
-    dw_part = pl.pallas_call(
-        weight_grad_kernel,
-        grid=(blocks,),
-        out_shape=jax.ShapeDtypeStruct((feat, width), BF16),
-        in_specs=[pl.BlockSpec((feat // blocks, tok), lambda i: (i, 0)), same, same, same],
-        out_specs=pl.BlockSpec((feat // blocks, width), lambda i: (i, 0)),
-        compiler_params=params,
-    )(x, dv_own, r1, r2)
 
     dw_block = swap_all(dw_part, YX_GROUPS)
     out, dq, dk_own, dk12, dk34 = pl.pallas_call(
         functools.partial(attention_kernel, factor),
         out_shape=[jax.ShapeDtypeStruct((tok, group * width), BF16)] * 2 + grads_shape,
-        in_specs=[smem] + [vmem] * 12,
+        in_specs=[smem] + [hbm] * 6 + [anywhere] * 4 + [vmem] * 2,
         out_specs=[vmem] * 5,
         scratch_shapes=[
+            pltpu.VMEM((tok, group * width), BF16),
+            pltpu.VMEM((tok, group * width), BF16),
             pltpu.VMEM((window, width), BF16),
             pltpu.VMEM((window, width), BF16),
             pltpu.VMEM((window, width), F32),
+            pltpu.SemaphoreType.DMA((12,)),
         ],
         compiler_params=params,
     )(base, q, do, k0, k1, k2, k34, v0, v1, v2, v34, start, lse)
@@ -269,12 +289,19 @@
         in_specs=[vmem, anywhere],
         out_specs=vmem,
         compiler_params=params,
+        cost_estimate=pl.CostEstimate(
+            flops=0, bytes_accessed=64 * 1024 * 1024, transcendentals=0
+        ),
     )(dw_own.reshape(Z, feat // (YX * Z), width), dk34)
     s1 = shifted(s1, -1)
     s2 = shifted(s2, -2)
-    d_keys = (
-        dk_own + s1.astype(F32) + s2.astype(F32)
-    ).astype(BF16)
+    d_keys = pl.pallas_call(
+        total_kernel,
+        out_shape=jax.ShapeDtypeStruct((tok, width), BF16),
+        in_specs=[vmem] * 3 + [anywhere],
+        out_specs=vmem,
+        compiler_params=params,
+    )(dk_own, s1, s2, projection_gradient)
     return (
         out[:, None, :],
         dq[:, None, :],

time: 162 us -> 157 us (0.969)
  the two profiles are of different devices: /device:TPU:40 before, /device:TPU:56 now
where the time goes in v3:
time: 157 us; the launch traced here: 156 us
  starting transfers between devices  63.4 us (40%)
  waiting for transfers between devices  32 us (20%)
  blocking collectives  19.2 us (12%)
  Pallas kernels  16.1 us (10%)
  between operations  15.1 us (10%)
  local copies, waits for them, and re-layouts  8.13 us (5%)
    ppermute x12, starting transfers between devices, shifted(): lax.ppermute(value, 'dp', [(source, source + steps) for source in range(f...  48.3 us
    ppermute x12, waiting for transfers between devices, shifted(): lax.ppermute(value, 'dp', [(source, source + steps) for source in range(f...  29.2 us
    all_to_all x1, blocking collectives, swap_all(): lax.all_to_all(value, 'dp', 0, 0, tiled=True, axis_index_groups=groups)  19.2 us
    all_to_all x3, starting transfers between devices, swap_all(): lax.all_to_all(value, 'dp', 0, 0, tiled=True, axis_index_groups=groups)  15.1 us
    unnamed x38, local copies, waits for them, and re-layouts  7 us
    pallas_call x1, Pallas kernels, body(): pl.pallas_call(functools.partial(attention_kernel, factor), out_shape=[ja...  6.96 us
    pallas_call x1, Pallas kernels, body(): pl.pallas_call(functools.partial(probs_kernel, factor), out_shape=[jax.Sh...  4.25 us
  transfers between devices with their start and end apart: 16, of which 8 were waited for; matrix products, arithmetic and copies ran while one was open for 2% of the time, Pallas kernels for 9%

profile of v3, /device:TPU:56, one launch (start us, length us, event | category | flops | bytes accessed | tf_op | source)
XLA Modules:
  0.0 156.4 jit_solution(11220172622234893459)
XLA Ops:
  8.7 19.2 %all_to_all.32 = bf16[8,64,128]{2,1,0:T(8,128)(2,1)S(1)} all-to-all(bf16[8,64,128]{2,1,0:T(8,128)(2,1)S(1)} %shard_map.110), channel_id=1, replica_groups={{0,8,16,24,32,40,48,56},{64,72,80,88,96,104,112,120},{128,136,144,152,1..., dimensions={0} | all-to-all | bytes 262144 | tf_op jit(solution)/shard_map/all_to_all | solution.py:32
  27.9 1.1 broadcast_in_dim.24
  29.1 5.8 %all-to-all-start.1 = ((bf16[8,512,128]{2,1,0:T(8,128)(2,1)}), bf16[8,512,128]{2,1,0:T(8,128)(2,1)S(1)}, u32[]{:S(2)}, u32[]{:S(2)}) async-start(bf16[8,512,128]{2,1,0:T(8,128)(2,1)} %broadcast_in_dim.24), calls=%async_computation.1 | async-start | bytes 2097152 | tf_op jit(solution)/shard_map/all_to_all | solution.py:32
  34.9 2.4 %collective-permute-start = (bf16[256,128]{1,0:T(8,128)(2,1)S(1)}, bf16[256,128]{1,0:T(8,128)(2,1)S(1)}, u32[]{:S(2)}, u32[]{:S(2)}) collective-permute-start(bf16[256,128]{1,0:T(8,128)(2,1)S(1)} %bitcast.26), channel_id=1, source_target_pairs={{0,8},{8,16},{16,24},{24,32},{32,40},{40,48},{48,56},{56,64},{64,7... | collective-permute-start | bytes 196616 | tf_op jit(solution)/shard_map/ppermute | solution.py:28
  37.3 2.6 %collective-permute-start.1 = (bf16[256,128]{1,0:T(8,128)(2,1)S(1)}, bf16[256,128]{1,0:T(8,128)(2,1)S(1)}, u32[]{:S(2)}, u32[]{:S(2)}) collective-permute-start(bf16[256,128]{1,0:T(8,128)(2,1)S(1)} %bitcast.27), channel_id=1, source_target_pairs={{0,16},{8,24},{16,32},{24,40},{32,48},{40,56},{48,64},{56,72},{64,... | collective-permute-start | bytes 196616 | tf_op jit(solution)/shard_map/ppermute | solution.py:28
  40.0 9.6 %collective-permute-done.k1 = bf16[256,128]{1,0:T(8,128)(2,1)S(1)} collective-permute-done((bf16[256,128]{1,0:T(8,128)(2,1)S(1)}, bf16[256,128]{1,0:T(8,128)(2,1)S(1)}, u32[]{:S(2)}, u32[]{:S(2)}) %collective-permute-start) | collective-permute-done | bytes 65568 | tf_op jit(solution)/shard_map/ppermute | solution.py:28
  51.0 1.9 %collective-permute-start.2 = (bf16[512,128]{1,0:T(8,128)(2,1)}, bf16[512,128]{1,0:T(8,128)(2,1)}, u32[]{:S(2)}, u32[]{:S(2)}) collective-permute-start(bf16[512,128]{1,0:T(8,128)(2,1)} %pad_maximum_fusion), channel_id=1, source_target_pairs={{0,16},{8,24},{16,32},{24,40},{32,48},{40,56},{48,64},{56,72},{64,... | collective-permute-start | bytes 393224 | tf_op jit(solution)/shard_map/ppermute | solution.py:28
  53.0 0.9 fusion.unused.v0
  53.9 3.6 %collective-permute-start.3 = (bf16[256,128]{1,0:T(8,128)(2,1)S(1)}, bf16[256,128]{1,0:T(8,128)(2,1)S(1)}, u32[]{:S(2)}, u32[]{:S(2)}) collective-permute-start(bf16[256,128]{1,0:T(8,128)(2,1)S(1)} %fusion.unused.v0), channel_id=1, source_target_pairs={{0,8},{8,16},{16,24},{24,32},{32,40},{40,48},{48,56},{56,64},{64,7... | collective-permute-start | bytes 196616 | tf_op jit(solution)/shard_map/ppermute | solution.py:28
  57.5 1.9 %collective-permute-start.4 = (bf16[256,128]{1,0:T(8,128)(2,1)S(1)}, bf16[256,128]{1,0:T(8,128)(2,1)}, u32[]{:S(2)}, u32[]{:S(2)}) collective-permute-start(bf16[256,128]{1,0:T(8,128)(2,1)S(1)} %fusion.unused.v0), channel_id=1, source_target_pairs={{0,16},{8,24},{16,32},{24,40},{32,48},{40,56},{48,64},{56,72},{64,... | collective-permute-start | bytes 196616 | tf_op jit(solution)/shard_map/ppermute | solution.py:28
  59.5 5.4 %collective-permute-done.2.k34 = bf16[512,128]{1,0:T(8,128)(2,1)} collective-permute-done((bf16[512,128]{1,0:T(8,128)(2,1)}, bf16[512,128]{1,0:T(8,128)(2,1)}, u32[]{:S(2)}, u32[]{:S(2)}) %collective-permute-start.2) | collective-permute-done | bytes 131104 | tf_op jit(solution)/shard_map/ppermute | solution.py:28
  64.8 0.9 copy-done.3
  65.8 0.8 copy-done.6
  68.3 4.3 %shard_map.111 = (f32[4,256]{1,0:T(4,128)S(1)}, f32[256,128]{1,0:T(8,128)S(1)}, f32[512,128]{1,0:T(8,128)S(1)}, bf16[512,128]{1,0:T(8,128)(2,1)S(1)}) custom-call(s32[1]{0:T(128)} %bitcast.base, bf16[256,512]{1,0:T(8,128)(2,1)S(1)} %bitcast.22, bf16[256,512]{1,0:T(8,128)(2,1)S(1)} %bitcast.24, bf16[256,128]{1,0:T(8,128)(2,1)S(1)} %bitcast.28, ...), custom_call_target="tpu_custom_call" | custom-call | tf_op jit(solution)/shard_map/pallas_call | solution.py:211
  72.6 3.7 %collective-permute-start.5 = (bf16[512,128]{1,0:T(8,128)(2,1)S(1)}, bf16[512,128]{1,0:T(8,128)(2,1)S(1)}, u32[]{:S(2)}, u32[]{:S(2)}) collective-permute-start(bf16[512,128]{1,0:T(8,128)(2,1)S(1)} %get-tuple-element.23), channel_id=1, source_target_pairs={{16,0},{24,8},{32,16},{40,24},{48,32},{56,40},{64,48},{72,56},{80,... | collective-permute-start | bytes 393224 | tf_op jit(solution)/shard_map/ppermute | solution.py:28
  76.3 0.9 pad_maximum_fusion.1
  77.1 3.1 %collective-permute-start.7 = (bf16[512,128]{1,0:T(8,128)(2,1)S(1)}, bf16[512,128]{1,0:T(8,128)(2,1)S(1)}, u32[]{:S(2)}, u32[]{:S(2)}) collective-permute-start(bf16[512,128]{1,0:T(8,128)(2,1)S(1)} %pad_maximum_fusion.1), channel_id=1, source_target_pairs={{0,16},{8,24},{16,32},{24,40},{32,48},{40,56},{48,64},{56,72},{64,... | collective-permute-start | bytes 393224 | tf_op jit(solution)/shard_map/ppermute | solution.py:28
  80.2 0.9 collective-permute-done.5.r34
  81.2 7.6 %collective-permute-start.6 = (bf16[256,128]{1,0:T(8,128)(2,1)S(1)}, bf16[256,128]{1,0:T(8,128)(2,1)S(1)}, u32[]{:S(2)}, u32[]{:S(2)}) collective-permute-start(bf16[256,128]{1,0:T(8,128)(2,1)S(1)} %get-tuple-element.24), channel_id=1, source_target_pairs={{8,0},{16,8},{24,16},{32,24},{40,32},{48,40},{56,48},{64,56},{72,6... | collective-permute-start | bytes 196616 | tf_op jit(solution)/shard_map/ppermute | solution.py:28
  88.8 2.4 %collective-permute-start.9 = (bf16[256,128]{1,0:T(8,128)(2,1)S(1)}, bf16[256,128]{1,0:T(8,128)(2,1)S(1)}, u32[]{:S(2)}, u32[]{:S(2)}) collective-permute-start(bf16[256,128]{1,0:T(8,128)(2,1)S(1)} %get-tuple-element.34), channel_id=1, source_target_pairs={{16,0},{24,8},{32,16},{40,24},{48,32},{56,40},{64,48},{72,56},{80,... | collective-permute-start | bytes 196616 | tf_op jit(solution)/shard_map/ppermute | solution.py:28
  91.9 4.0 %collective-permute-done.9.r2 = bf16[256,128]{1,0:T(8,128)(2,1)S(1)} collective-permute-done((bf16[256,128]{1,0:T(8,128)(2,1)S(1)}, bf16[256,128]{1,0:T(8,128)(2,1)S(1)}, u32[]{:S(2)}, u32[]{:S(2)}) %collective-permute-start.9) | collective-permute-done | bytes 65568 | tf_op jit(solution)/shard_map/ppermute | solution.py:28
  95.8 2.7 %shard_map.114 = (bf16[4096,256]{1,0:T(8,128)(2,1)S(1)}, bf16[4096,128]{1,0:T(8,128)(2,1)}) custom-call(bf16[4096,256]{1,0:T(8,128)(2,1)S(1)} %copy-done, bf16[4096,128]{1,0:T(8,128)(2,1)S(1)} %bitcast.21, f32[256,128]{1,0:T(8,128)S(1)} %get-tuple-element.32.own, bf16[256,128]{1,0:T(8,128)(2,1)S(1)} %collective-permute-done.6.r1, ...), custom_call_target="tpu_custom_call" | custom-call | tf_op jit(solution)/shard_map/pallas_call | solution.py:248
  98.6 1.4 copy-done.1
  100.0 3.7 %all-to-all-start.2 = ((bf16[8,512,128]{2,1,0:T(8,128)(2,1)}), bf16[8,512,128]{2,1,0:T(8,128)(2,1)S(1)}, u32[]{:S(2)}, u32[]{:S(2)}) async-start(bf16[8,512,128]{2,1,0:T(8,128)(2,1)} %bitcast.11), calls=%async_computation.2 | async-start | bytes 2097152 | tf_op jit(solution)/shard_map/all_to_all | solution.py:32
  103.7 7.0 %shard_map.113 = (bf16[256,512]{1,0:T(8,128)(2,1)}, bf16[256,512]{1,0:T(8,128)(2,1)}, f32[256,128]{1,0:T(8,128)S(1)}, f32[512,128]{1,0:T(8,128)S(1)}, bf16[512,128]{1,0:T(8,128)(2,1)S(1)}) custom-call(s32[1]{0:T(128)} %bitcast.base, bf16[256,512]{1,0:T(8,128)(2,1)S(1)} %bitcast.23, bf16[256,512]{1,0:T(8,128)(2,1)S(1)} %bitcast.25, ...), custom_call_target="tpu_custom_call" | custom-call | tf_op jit(solution)/shard_map/pallas_call | solution.py:262
  110.7 2.8 %all-to-all-done.2.parts = bf16[8,512,128]{2,1,0:T(8,128)(2,1)S(1)} async-done(((bf16[8,512,128]{2,1,0:T(8,128)(2,1)}), bf16[8,512,128]{2,1,0:T(8,128)(2,1)S(1)}, u32[]{:S(2)}, u32[]{:S(2)}) %all-to-all-start.2) | async-done | bytes 1048608 | tf_op jit(solution)/shard_map/all_to_all | solution.py:32
  114.3 5.7 %all-to-all-start.3 = ((bf16[8,64,128]{2,1,0:T(8,128)(2,1)}), bf16[8,64,128]{2,1,0:T(8,128)(2,1)S(1)}, u32[]{:S(2)}, u32[]{:S(2)}) async-start(bf16[8,64,128]{2,1,0:T(8,128)(2,1)} %bitcast.12), calls=%async_computation.3 | async-start | bytes 262144 | tf_op jit(solution)/shard_map/all_to_all | solution.py:32
  119.9 7.4 %collective-permute-start.8 = (bf16[512,128]{1,0:T(8,128)(2,1)S(1)}, bf16[512,128]{1,0:T(8,128)(2,1)S(1)}, u32[]{:S(2)}, u32[]{:S(2)}) collective-permute-start(bf16[512,128]{1,0:T(8,128)(2,1)S(1)} %get-tuple-element.31.unused), channel_id=1, source_target_pairs={{16,0},{24,8},{32,16},{40,24},{48,32},{56,40},{64,48},{72,56},{80,... | collective-permute-start | bytes 393224 | tf_op jit(solution)/shard_map/ppermute | solution.py:28
  127.3 4.6 %collective-permute-done.8.r34 = bf16[512,128]{1,0:T(8,128)(2,1)S(1)} collective-permute-done((bf16[512,128]{1,0:T(8,128)(2,1)S(1)}, bf16[512,128]{1,0:T(8,128)(2,1)S(1)}, u32[]{:S(2)}, u32[]{:S(2)}) %collective-permute-start.8) | collective-permute-done | bytes 131104 | tf_op jit(solution)/shard_map/ppermute | solution.py:28
  131.9 9.1 %collective-permute-start.10 = (bf16[256,128]{1,0:T(8,128)(2,1)S(1)}, bf16[256,128]{1,0:T(8,128)(2,1)S(1)}, u32[]{:S(2)}, u32[]{:S(2)}) collective-permute-start(bf16[256,128]{1,0:T(8,128)(2,1)S(1)} %get-tuple-element.36), channel_id=1, source_target_pairs={{8,0},{16,8},{24,16},{32,24},{40,32},{48,40},{56,48},{64,56},{72,6... | collective-permute-start | bytes 196616 | tf_op jit(solution)/shard_map/ppermute | solution.py:28
  141.1 2.5 %collective-permute-start.11 = (bf16[256,128]{1,0:T(8,128)(2,1)S(1)}, bf16[256,128]{1,0:T(8,128)(2,1)S(1)}, u32[]{:S(2)}, u32[]{:S(2)}) collective-permute-start(bf16[256,128]{1,0:T(8,128)(2,1)S(1)} %get-tuple-element.37), channel_id=1, source_target_pairs={{16,0},{24,8},{32,16},{40,24},{48,32},{56,40},{64,48},{72,56},{80,... | collective-permute-start | bytes 196616 | tf_op jit(solution)/shard_map/ppermute | solution.py:28
  144.2 3.9 %collective-permute-done.11.r2 = bf16[256,128]{1,0:T(8,128)(2,1)S(1)} collective-permute-done((bf16[256,128]{1,0:T(8,128)(2,1)S(1)}, bf16[256,128]{1,0:T(8,128)(2,1)S(1)}, u32[]{:S(2)}, u32[]{:S(2)}) %collective-permute-start.11) | collective-permute-done | bytes 65568 | tf_op jit(solution)/shard_map/ppermute | solution.py:28
  (53 shorter events, 7.5 us)
Async XLA Ops:
  7.2 27.7 %copy-start.11 = (bf16[256,1,128]{2,0,1:T(8,128)(2,1)S(1)}, bf16[256,1,128]{2,0,1:T(8,128)(2,1)}, u32[]{:S(2)}) copy-start(bf16[256,1,128]{2,0,1:T(8,128)(2,1)} %param.11) | copy-start | bytes 196612
  7.2 45.8 %copy-start = (bf16[4096,256]{1,0:T(8,128)(2,1)S(1)}, bf16[4096,256]{1,0:T(8,128)(2,1)}, u32[]{:S(2)}) copy-start(bf16[4096,256]{1,0:T(8,128)(2,1)} %x.1) | copy-start | bytes 6291460
  29.1 23.9 %all-to-all-start.1 = ((bf16[8,512,128]{2,1,0:T(8,128)(2,1)}), bf16[8,512,128]{2,1,0:T(8,128)(2,1)S(1)}, u32[]{:S(2)}, u32[]{:S(2)}) async-start(bf16[8,512,128]{2,1,0:T(8,128)(2,1)} %broadcast_in_dim.24), calls=%async_computation.1 | async-start | bytes 2097152 | tf_op jit(solution)/shard_map/all_to_all | solution.py:32
  34.8 30.0 %copy-start.2 = (bf16[256,1,512]{2,0,1:T(8,128)(2,1)S(1)}, bf16[256,1,512]{2,0,1:T(8,128)(2,1)}, u32[]{:S(2)}) copy-start(bf16[256,1,512]{2,0,1:T(8,128)(2,1)} %param.10) | copy-start | bytes 786436
  34.8 30.0 %copy-start.18 = (s32[256]{0:T(256)S(1)}, s32[256]{0:T(256)}, u32[]{:S(2)}) copy-start(s32[256]{0:T(256)} %param.12) | copy-start | bytes 3076
  34.8 114.7 %reduce-scatter.2.cloned.1.call-start = ((), (), s32[]{:S(2)}) async-start(), calls=%async_computation.5 | async-start | bytes 2359296 | tf_op jit(solution)/shard_map/reduce_scatter | solution.py:259
  34.9 14.7 %collective-permute-start = (bf16[256,128]{1,0:T(8,128)(2,1)S(1)}, bf16[256,128]{1,0:T(8,128)(2,1)S(1)}, u32[]{:S(2)}, u32[]{:S(2)}) collective-permute-start(bf16[256,128]{1,0:T(8,128)(2,1)S(1)} %bitcast.26), channel_id=1, source_target_pairs={{0,8},{8,16},{16,24},{24,32},{32,40},{40,48},{48,56},{56,64},{64,7... | collective-permute-start | bytes 196616 | tf_op jit(solution)/shard_map/ppermute | solution.py:28
  37.3 13.0 %collective-permute-start.1 = (bf16[256,128]{1,0:T(8,128)(2,1)S(1)}, bf16[256,128]{1,0:T(8,128)(2,1)S(1)}, u32[]{:S(2)}, u32[]{:S(2)}) collective-permute-start(bf16[256,128]{1,0:T(8,128)(2,1)S(1)} %bitcast.27), channel_id=1, source_target_pairs={{0,16},{8,24},{16,32},{24,40},{32,48},{40,56},{48,64},{56,72},{64,... | collective-permute-start | bytes 196616 | tf_op jit(solution)/shard_map/ppermute | solution.py:28
  49.5 1.5 copy-start.5
  51.0 13.8 %collective-permute-start.2 = (bf16[512,128]{1,0:T(8,128)(2,1)}, bf16[512,128]{1,0:T(8,128)(2,1)}, u32[]{:S(2)}, u32[]{:S(2)}) collective-permute-start(bf16[512,128]{1,0:T(8,128)(2,1)} %pad_maximum_fusion), channel_id=1, source_target_pairs={{0,16},{8,24},{16,32},{24,40},{32,48},{40,56},{48,64},{56,72},{64,... | collective-permute-start | bytes 393224 | tf_op jit(solution)/shard_map/ppermute | solution.py:28
  53.9 22.4 %collective-permute-start.3 = (bf16[256,128]{1,0:T(8,128)(2,1)S(1)}, bf16[256,128]{1,0:T(8,128)(2,1)S(1)}, u32[]{:S(2)}, u32[]{:S(2)}) collective-permute-start(bf16[256,128]{1,0:T(8,128)(2,1)S(1)} %fusion.unused.v0), channel_id=1, source_target_pairs={{0,8},{8,16},{16,24},{24,32},{32,40},{40,48},{48,56},{56,64},{64,7... | collective-permute-start | bytes 196616 | tf_op jit(solution)/shard_map/ppermute | solution.py:28
  57.5 18.8 %collective-permute-start.4 = (bf16[256,128]{1,0:T(8,128)(2,1)S(1)}, bf16[256,128]{1,0:T(8,128)(2,1)}, u32[]{:S(2)}, u32[]{:S(2)}) collective-permute-start(bf16[256,128]{1,0:T(8,128)(2,1)S(1)} %fusion.unused.v0), channel_id=1, source_target_pairs={{0,16},{8,24},{16,32},{24,40},{32,48},{40,56},{48,64},{56,72},{64,... | collective-permute-start | bytes 196616 | tf_op jit(solution)/shard_map/ppermute | solution.py:28
  64.8 1.0 copy-start.3
  65.8 0.8 copy-start.6
  66.6 0.8 copy-start.9
  67.5 0.8 copy-start.12
  72.6 8.6 %collective-permute-start.5 = (bf16[512,128]{1,0:T(8,128)(2,1)S(1)}, bf16[512,128]{1,0:T(8,128)(2,1)S(1)}, u32[]{:S(2)}, u32[]{:S(2)}) collective-permute-start(bf16[512,128]{1,0:T(8,128)(2,1)S(1)} %get-tuple-element.23), channel_id=1, source_target_pairs={{16,0},{24,8},{32,16},{40,24},{48,32},{56,40},{64,48},{72,56},{80,... | collective-permute-start | bytes 393224 | tf_op jit(solution)/shard_map/ppermute | solution.py:28
  77.1 14.1 %collective-permute-start.7 = (bf16[512,128]{1,0:T(8,128)(2,1)S(1)}, bf16[512,128]{1,0:T(8,128)(2,1)S(1)}, u32[]{:S(2)}, u32[]{:S(2)}) collective-permute-start(bf16[512,128]{1,0:T(8,128)(2,1)S(1)} %pad_maximum_fusion.1), channel_id=1, source_target_pairs={{0,16},{8,24},{16,32},{24,40},{32,48},{40,56},{48,64},{56,72},{64,... | collective-permute-start | bytes 393224 | tf_op jit(solution)/shard_map/ppermute | solution.py:28
  81.2 10.0 %collective-permute-start.6 = (bf16[256,128]{1,0:T(8,128)(2,1)S(1)}, bf16[256,128]{1,0:T(8,128)(2,1)S(1)}, u32[]{:S(2)}, u32[]{:S(2)}) collective-permute-start(bf16[256,128]{1,0:T(8,128)(2,1)S(1)} %get-tuple-element.24), channel_id=1, source_target_pairs={{8,0},{16,8},{24,16},{32,24},{40,32},{48,40},{56,48},{64,56},{72,6... | collective-permute-start | bytes 196616 | tf_op jit(solution)/shard_map/ppermute | solution.py:28
  88.8 7.1 %collective-permute-start.9 = (bf16[256,128]{1,0:T(8,128)(2,1)S(1)}, bf16[256,128]{1,0:T(8,128)(2,1)S(1)}, u32[]{:S(2)}, u32[]{:S(2)}) collective-permute-start(bf16[256,128]{1,0:T(8,128)(2,1)S(1)} %get-tuple-element.34), channel_id=1, source_target_pairs={{16,0},{24,8},{32,16},{40,24},{48,32},{56,40},{64,48},{72,56},{80,... | collective-permute-start | bytes 196616 | tf_op jit(solution)/shard_map/ppermute | solution.py:28
  98.6 1.4 copy-start.1
  99.9 3.7 %copy-start.4 = (bf16[256,1,512]{2,0,1:T(8,128)(2,1)S(1)}, bf16[256,1,512]{2,0,1:T(8,128)(2,1)}, u32[]{:S(2)}) copy-start(bf16[256,1,512]{2,0,1:T(8,128)(2,1)} %param.13) | copy-start | bytes 786436
  99.9 3.7 %copy-start.7 = (bf16[256,128]{1,0:T(8,128)(2,1)S(1)}, bf16[256,128]{1,0:T(8,128)(2,1)}, u32[]{:S(2)}) copy-start(bf16[256,128]{1,0:T(8,128)(2,1)} %copy-done.5) | copy-start | bytes 196612
  99.9 3.7 %copy-start.10 = (bf16[256,128]{1,0:T(8,128)(2,1)S(1)}, bf16[256,128]{1,0:T(8,128)(2,1)}, u32[]{:S(2)}) copy-start(bf16[256,128]{1,0:T(8,128)(2,1)} %copy-done.8) | copy-start | bytes 196612
  99.9 3.7 %copy-start.13 = (bf16[256,1,128]{2,0,1:T(8,128)(2,1)S(1)}, bf16[256,1,128]{2,0,1:T(8,128)(2,1)}, u32[]{:S(2)}) copy-start(bf16[256,1,128]{2,0,1:T(8,128)(2,1)} %param.11) | copy-start | bytes 196612
  99.9 3.7 %copy-start.15 = (bf16[512,128]{1,0:T(8,128)(2,1)S(1)}, bf16[512,128]{1,0:T(8,128)(2,1)}, u32[]{:S(2)}) copy-start(bf16[512,128]{1,0:T(8,128)(2,1)} %copy-done.14) | copy-start | bytes 393220
  100.0 13.5 %all-to-all-start.2 = ((bf16[8,512,128]{2,1,0:T(8,128)(2,1)}), bf16[8,512,128]{2,1,0:T(8,128)(2,1)S(1)}, u32[]{:S(2)}, u32[]{:S(2)}) async-start(bf16[8,512,128]{2,1,0:T(8,128)(2,1)} %bitcast.11), calls=%async_computation.2 | async-start | bytes 2097152 | tf_op jit(solution)/shard_map/all_to_all | solution.py:32
  114.3 29.3 %all-to-all-start.3 = ((bf16[8,64,128]{2,1,0:T(8,128)(2,1)}), bf16[8,64,128]{2,1,0:T(8,128)(2,1)S(1)}, u32[]{:S(2)}, u32[]{:S(2)}) async-start(bf16[8,64,128]{2,1,0:T(8,128)(2,1)} %bitcast.12), calls=%async_computation.3 | async-start | bytes 262144 | tf_op jit(solution)/shard_map/all_to_all | solution.py:32
  119.9 12.0 %collective-permute-start.8 = (bf16[512,128]{1,0:T(8,128)(2,1)S(1)}, bf16[512,128]{1,0:T(8,128)(2,1)S(1)}, u32[]{:S(2)}, u32[]{:S(2)}) collective-permute-start(bf16[512,128]{1,0:T(8,128)(2,1)S(1)} %get-tuple-element.31.unused), channel_id=1, source_target_pairs={{16,0},{24,8},{32,16},{40,24},{48,32},{56,40},{64,48},{72,56},{80,... | collective-permute-start | bytes 393224 | tf_op jit(solution)/shard_map/ppermute | solution.py:28
  131.9 12.3 %collective-permute-start.10 = (bf16[256,128]{1,0:T(8,128)(2,1)S(1)}, bf16[256,128]{1,0:T(8,128)(2,1)S(1)}, u32[]{:S(2)}, u32[]{:S(2)}) collective-permute-start(bf16[256,128]{1,0:T(8,128)(2,1)S(1)} %get-tuple-element.36), channel_id=1, source_target_pairs={{8,0},{16,8},{24,16},{32,24},{40,32},{48,40},{56,48},{64,56},{72,6... | collective-permute-start | bytes 196616 | tf_op jit(solution)/shard_map/ppermute | solution.py:28
  141.1 7.1 %collective-permute-start.11 = (bf16[256,128]{1,0:T(8,128)(2,1)S(1)}, bf16[256,128]{1,0:T(8,128)(2,1)S(1)}, u32[]{:S(2)}, u32[]{:S(2)}) collective-permute-start(bf16[256,128]{1,0:T(8,128)(2,1)S(1)} %get-tuple-element.37), channel_id=1, source_target_pairs={{16,0},{24,8},{32,16},{40,24},{48,32},{56,40},{64,48},{72,56},{80,... | collective-permute-start | bytes 196616 | tf_op jit(solution)/shard_map/ppermute | solution.py:28
  148.1 0.8 copy-start.16
  (3 other events, 2.1 us)
Sparse Core Ops, SparseCore 0:
  100.1 39.6 reduce-scatter.1

commit v4 on v3

--- a/solution.py
+++ b/solution.py
@@ -42,14 +42,11 @@
     return lax.dot_general(a, b, dims, preferred_element_type=F32)
 
 
-def window_parts(win, own, h1, h2, h34):
+def window_parts(win, own, *earlier):
     tok = own.shape[0]
     return [
-        (own, win.at[4 * tok : 5 * tok]),
-        (h1, win.at[3 * tok : 4 * tok]),
-        (h2, win.at[2 * tok : 3 * tok]),
-        (h34.at[0:tok], win.at[tok : 2 * tok]),
-        (h34.at[tok : 2 * tok], win.at[0:tok]),
+        (ref, win.at[(SPAN - i) * tok : (SPAN - i + 1) * tok])
+        for i, ref in enumerate((own, *earlier))
     ]
 
 
@@ -86,12 +83,19 @@
     g34[tok:] = acc[0:tok].astype(BF16)
 
 
+def store_each(acc, own, *earlier):
+    tok = own.shape[0]
+    own[...] = acc[SPAN * tok :]
+    for i, ref in enumerate(earlier):
+        ref[...] = acc[(SPAN - 1 - i) * tok : (SPAN - i) * tok].astype(BF16)
+
+
 def probs_kernel(
-    factor, base, q_in, do_in, k0, k1, k2, k34, start, unused, lse, dv_own, dv12, dv34,
+    factor, base, q_in, do_in, k0, k1, k2, k3, k4, start, unused, lse, dv_own, dv12, dv34,
     q, do, kwin, acc, sems,
 ):
     width = k0.shape[1]
-    fetch([(q_in, q), (do_in, do)] + window_parts(kwin, k0, k1, k2, k34), sems)
+    fetch([(q_in, q), (do_in, do)] + window_parts(kwin, k0, k1, k2, k3, k4), sems)
     for g in range(q.shape[1] // width):
         cols = slice(g * width, (g + 1) * width)
         scores = masked_scores(factor, base[0], kwin[...], q[:, cols], start[...])
@@ -105,14 +109,14 @@
 
 
 def attention_kernel(
-    factor, base, q_in, do_in, k0, k1, k2, k34, v0, v1, v2, v34, start, lse,
-    out, dq, dk_own, dk12, dk34, q, do, kwin, vwin, acc, sems,
+    factor, base, q_in, do_in, k0, k1, k2, k3, k4, v0, v1, v2, v34, start, lse,
+    out, dq, dk_own, dk1, dk2, dk3, dk4, q, do, kwin, vwin, acc, sems,
 ):
-    width = k0.shape[1]
+    tok, width = k0.shape
     fetch(
         [(q_in, q), (do_in, do)]
-        + window_parts(kwin, k0, k1, k2, k34)
-        + window_parts(vwin, v0, v1, v2, v34),
+        + window_parts(kwin, k0, k1, k2, k3, k4)
+        + window_parts(vwin, v0, v1, v2, v34.at[0:tok], v34.at[tok : 2 * tok]),
         sems,
     )
     k_cols = kwin[...].T
@@ -129,7 +133,7 @@
         ds = (p.astype(F32) * (dprob - delta) * factor).astype(BF16)
         dq[:, cols] = mm(k_cols, ds, NN).T.astype(BF16)
         add_to(acc, mm(ds, q[:, cols], NN), g == 0)
-    store_grads(acc, dk_own, dk12, dk34)
+    store_each(acc, dk_own, dk1, dk2, dk3, dk4)
 
 
 def weight_copies_kernel(exponent, codes, out):
@@ -154,8 +158,11 @@
     near2[...] = (g12[tok:] + r34[tok:].astype(F32)).astype(BF16)
 
 
-def total_kernel(own, r1, r2, unused, out):
-    out[...] = (own[...] + r1[...].astype(F32) + r2[...].astype(F32)).astype(BF16)
+def total_kernel(own, r1, r2, r3, r4, unused, out):
+    total = own[...]
+    for ref in (r1, r2, r3, r4):
+        total = total + ref[...].astype(F32)
+    out[...] = total.astype(BF16)
 
 
 def sum_kernel(parts, unused, out):
@@ -196,7 +203,8 @@
     k1 = shifted(k0, 1)
     k2 = shifted(k0, 2)
     w_full = swap_all(copies(w_block, YX), YX_GROUPS)
-    k34 = shifted(jnp.concatenate([k1, k2], axis=0), 2)
+    k3 = shifted(k0, 3)
+    k4 = shifted(k0, 4)
     v0 = lax.dot_general(
         x, w_full, (((0,), (0,)), ((), ())), preferred_element_type=F32
     ).astype(BF16)
@@ -211,7 +219,7 @@
     lse, dv_own, dv12, dv34 = pl.pallas_call(
         functools.partial(probs_kernel, factor),
         out_shape=[jax.ShapeDtypeStruct((group, tok), F32)] + grads_shape,
-        in_specs=[smem] + [hbm] * 6 + [vmem, anywhere],
+        in_specs=[smem] + [hbm] * 7 + [vmem, anywhere],
         out_specs=[vmem] * 4,
         scratch_shapes=[
             pltpu.VMEM((tok, group * width), BF16),
@@ -221,7 +229,7 @@
             pltpu.SemaphoreType.DMA((7,)),
         ],
         compiler_params=params,
-    )(base, q, do, k0, k1, k2, k34, start, v0)
+    )(base, q, do, k0, k1, k2, k3, k4, start, v0)
 
 
     def near_sum(g12, r34, unused):
@@ -259,11 +267,13 @@
     d_input = lax.psum_scatter(d_part, "tensor", scatter_dimension=0, tiled=True)
 
     dw_block = swap_all(dw_part, YX_GROUPS)
-    out, dq, dk_own, dk12, dk34 = pl.pallas_call(
+    out, dq, dk_own, *dk_earlier = pl.pallas_call(
         functools.partial(attention_kernel, factor),
-        out_shape=[jax.ShapeDtypeStruct((tok, group * width), BF16)] * 2 + grads_shape,
-        in_specs=[smem] + [hbm] * 6 + [anywhere] * 4 + [vmem] * 2,
-        out_specs=[vmem] * 5,
+        out_shape=[jax.ShapeDtypeStruct((tok, group * width), BF16)] * 2
+        + [jax.ShapeDtypeStruct((tok, width), F32)]
+        + [jax.ShapeDtypeStruct((tok, width), BF16)] * SPAN,
+        in_specs=[smem] + [hbm] * 7 + [anywhere] * 4 + [vmem] * 2,
+        out_specs=[vmem] * (3 + SPAN),
         scratch_shapes=[
             pltpu.VMEM((tok, group * width), BF16),
             pltpu.VMEM((tok, group * width), BF16),
@@ -273,16 +283,15 @@
             pltpu.SemaphoreType.DMA((12,)),
         ],
         compiler_params=params,
-    )(base, q, do, k0, k1, k2, k34, v0, v1, v2, v34, start, lse)
+    )(base, q, do, k0, k1, k2, k3, k4, v0, v1, v2, v34, start, lse)
     dw_block = pl.pallas_call(
         sum_kernel,
         out_shape=jax.ShapeDtypeStruct((feat // YX, width), BF16),
         in_specs=[vmem, anywhere],
         out_specs=vmem,
         compiler_params=params,
-    )(dw_block.reshape(YX, feat // YX, width), dk34)
+    )(dw_block.reshape(YX, feat // YX, width), dk_own)
     dw_own = swap_all(dw_block, Z_GROUPS)
-    s1, s2 = near_sum(dk12, shifted(dk34, -2), dw_block)
     projection_gradient = pl.pallas_call(
         sum_kernel,
         out_shape=jax.ShapeDtypeStruct((feat // (YX * Z), width), F32),
@@ -292,16 +301,15 @@
         cost_estimate=pl.CostEstimate(
             flops=0, bytes_accessed=64 * 1024 * 1024, transcendentals=0
         ),
-    )(dw_own.reshape(Z, feat // (YX * Z), width), dk34)
-    s1 = shifted(s1, -1)
-    s2 = shifted(s2, -2)
+    )(dw_own.reshape(Z, feat // (YX * Z), width), dk_own)
+    dk_far = [shifted(grad, -1 - i) for i, grad in enumerate(dk_earlier)]
     d_keys = pl.pallas_call(
         total_kernel,
         out_shape=jax.ShapeDtypeStruct((tok, width), BF16),
-        in_specs=[vmem] * 3 + [anywhere],
+        in_specs=[vmem] * (1 + SPAN) + [anywhere],
         out_specs=vmem,
         compiler_params=params,
-    )(dk_own, s1, s2, projection_gradient)
+    )(dk_own, *dk_far, projection_gradient)
     return (
         out[:, None, :],
         dq[:, None, :],

time: 157 us -> 148 us (0.943)
  the two profiles are of different devices: /device:TPU:56 before, /device:TPU:25 now
where the time goes in v4:
time: 148 us; the launch traced here: 147 us
  starting transfers between devices  72.6 us (49%)
  waiting for transfers between devices  18.9 us (13%)
  blocking collectives  17.6 us (12%)
  Pallas kernels  15.8 us (11%)
  between operations  15.1 us (10%)
  local copies, waits for them, and re-layouts  5.56 us (4%)
    ppermute x14, starting transfers between devices, shifted(): lax.ppermute(value, 'dp', [(source, source + steps) for source in range(f...  57.9 us
    all_to_all x1, blocking collectives, swap_all(): lax.all_to_all(value, 'dp', 0, 0, tiled=True, axis_index_groups=groups)  17.6 us
    all_to_all x3, starting transfers between devices, swap_all(): lax.all_to_all(value, 'dp', 0, 0, tiled=True, axis_index_groups=groups)  14.7 us
    reduce_scatter x1, waiting for transfers between devices, body(): lax.psum_scatter(d_part, 'tensor', scatter_dimension=0, tiled=True)  9.09 us
    ppermute x14, waiting for transfers between devices, shifted(): lax.ppermute(value, 'dp', [(source, source + steps) for source in range(f...  6.92 us
    pallas_call x1, Pallas kernels, body(): pl.pallas_call(functools.partial(attention_kernel, factor), out_shape=[ja...  6.75 us
    unnamed x20, local copies, waits for them, and re-layouts  4.44 us
    pallas_call x1, Pallas kernels, body(): pl.pallas_call(functools.partial(probs_kernel, factor), out_shape=[jax.Sh...  4.09 us
  transfers between devices with their start and end apart: 18, of which 7 were waited for; matrix products, arithmetic and copies ran while one was open for 1% of the time, Pallas kernels for 9%

profile of v4, /device:TPU:25, one launch (start us, length us, event | category | flops | bytes accessed | tf_op | source)
XLA Modules:
  0.0 147.3 jit_solution(12311473822718143738)
XLA Ops:
  8.7 17.6 %all_to_all.32 = bf16[8,64,128]{2,1,0:T(8,128)(2,1)S(1)} all-to-all(bf16[8,64,128]{2,1,0:T(8,128)(2,1)S(1)} %shard_map.110), channel_id=1, replica_groups={{0,8,16,24,32,40,48,56},{64,72,80,88,96,104,112,120},{128,136,144,152,1..., dimensions={0} | all-to-all | bytes 262144 | tf_op jit(solution)/shard_map/all_to_all | solution.py:32
  26.3 1.1 broadcast_in_dim.24
  27.4 5.2 %all-to-all-start.1 = ((bf16[8,512,128]{2,1,0:T(8,128)(2,1)}), bf16[8,512,128]{2,1,0:T(8,128)(2,1)S(1)}, u32[]{:S(2)}, u32[]{:S(2)}) async-start(bf16[8,512,128]{2,1,0:T(8,128)(2,1)} %broadcast_in_dim.24), calls=%async_computation.1 | async-start | bytes 2097152 | tf_op jit(solution)/shard_map/all_to_all | solution.py:32
  32.7 2.5 %collective-permute-start = (bf16[256,128]{1,0:T(8,128)(2,1)}, bf16[256,128]{1,0:T(8,128)(2,1)}, u32[]{:S(2)}, u32[]{:S(2)}) collective-permute-start(bf16[256,128]{1,0:T(8,128)(2,1)} %bitcast.3.k0), channel_id=1, source_target_pairs={{0,8},{8,16},{16,24},{24,32},{32,40},{40,48},{48,56},{56,64},{64,7... | collective-permute-start | bytes 196616 | tf_op jit(solution)/shard_map/ppermute | solution.py:28
  35.2 2.0 %collective-permute-start.1 = (bf16[256,128]{1,0:T(8,128)(2,1)}, bf16[256,128]{1,0:T(8,128)(2,1)}, u32[]{:S(2)}, u32[]{:S(2)}) collective-permute-start(bf16[256,128]{1,0:T(8,128)(2,1)} %bitcast.3.k0), channel_id=1, source_target_pairs={{0,16},{8,24},{16,32},{24,40},{32,48},{40,56},{48,64},{56,72},{64,... | collective-permute-start | bytes 196616 | tf_op jit(solution)/shard_map/ppermute | solution.py:28
  37.2 4.7 %collective-permute-start.2 = (bf16[256,128]{1,0:T(8,128)(2,1)}, bf16[256,128]{1,0:T(8,128)(2,1)}, u32[]{:S(2)}, u32[]{:S(2)}) collective-permute-start(bf16[256,128]{1,0:T(8,128)(2,1)} %bitcast.3.k0), channel_id=1, source_target_pairs={{0,24},{8,32},{16,40},{24,48},{32,56},{40,64},{48,72},{56,80},{64,... | collective-permute-start | bytes 196616 | tf_op jit(solution)/shard_map/ppermute | solution.py:28
  42.0 5.2 %collective-permute-start.3 = (bf16[256,128]{1,0:T(8,128)(2,1)}, bf16[256,128]{1,0:T(8,128)(2,1)}, u32[]{:S(2)}, u32[]{:S(2)}) collective-permute-start(bf16[256,128]{1,0:T(8,128)(2,1)} %bitcast.3.k0), channel_id=1, source_target_pairs={{0,32},{8,40},{16,48},{24,56},{32,64},{40,72},{48,80},{56,88},{64,... | collective-permute-start | bytes 196616 | tf_op jit(solution)/shard_map/ppermute | solution.py:28
  47.2 1.2 all-to-all-done.1
  48.4 0.9 fusion.unused.v0
  49.4 1.9 %collective-permute-start.4 = (bf16[256,128]{1,0:T(8,128)(2,1)S(1)}, bf16[256,128]{1,0:T(8,128)(2,1)S(1)}, u32[]{:S(2)}, u32[]{:S(2)}) collective-permute-start(bf16[256,128]{1,0:T(8,128)(2,1)S(1)} %fusion.unused.v0), channel_id=1, source_target_pairs={{0,8},{8,16},{16,24},{24,32},{32,40},{40,48},{48,56},{56,64},{64,7... | collective-permute-start | bytes 196616 | tf_op jit(solution)/shard_map/ppermute | solution.py:28
  51.3 2.4 %collective-permute-start.5 = (bf16[256,128]{1,0:T(8,128)(2,1)S(1)}, bf16[256,128]{1,0:T(8,128)(2,1)}, u32[]{:S(2)}, u32[]{:S(2)}) collective-permute-start(bf16[256,128]{1,0:T(8,128)(2,1)S(1)} %fusion.unused.v0), channel_id=1, source_target_pairs={{0,16},{8,24},{16,32},{24,40},{32,48},{40,56},{48,64},{56,72},{64,... | collective-permute-start | bytes 196616 | tf_op jit(solution)/shard_map/ppermute | solution.py:28
  54.4 0.9 copy-done.3
  55.3 4.1 %shard_map.111 = (f32[4,256]{1,0:T(4,128)S(1)}, f32[256,128]{1,0:T(8,128)S(1)}, f32[512,128]{1,0:T(8,128)S(1)}, bf16[512,128]{1,0:T(8,128)(2,1)S(1)}) custom-call(s32[1]{0:T(128)} %bitcast.base, bf16[256,512]{1,0:T(8,128)(2,1)S(1)} %bitcast.22, bf16[256,512]{1,0:T(8,128)(2,1)S(1)} %bitcast.24, bf16[256,128]{1,0:T(8,128)(2,1)} %bitcast.3.k0, ...), custom_call_target="tpu_custom_call" | custom-call | tf_op jit(solution)/shard_map/pallas_call | solution.py:219
  59.4 7.4 %collective-permute-start.6 = (bf16[512,128]{1,0:T(8,128)(2,1)S(1)}, bf16[512,128]{1,0:T(8,128)(2,1)S(1)}, u32[]{:S(2)}, u32[]{:S(2)}) collective-permute-start(bf16[512,128]{1,0:T(8,128)(2,1)S(1)} %get-tuple-element.23), channel_id=1, source_target_pairs={{16,0},{24,8},{32,16},{40,24},{48,32},{56,40},{64,48},{72,56},{80,... | collective-permute-start | bytes 393224 | tf_op jit(solution)/shard_map/ppermute | solution.py:28
  66.9 0.9 pad_maximum_fusion
  67.7 1.9 %collective-permute-start.8 = (bf16[512,128]{1,0:T(8,128)(2,1)S(1)}, bf16[512,128]{1,0:T(8,128)(2,1)S(1)}, u32[]{:S(2)}, u32[]{:S(2)}) collective-permute-start(bf16[512,128]{1,0:T(8,128)(2,1)S(1)} %pad_maximum_fusion), channel_id=1, source_target_pairs={{0,16},{8,24},{16,32},{24,40},{32,48},{40,56},{48,64},{56,72},{64,... | collective-permute-start | bytes 393224 | tf_op jit(solution)/shard_map/ppermute | solution.py:28
  69.7 8.4 %collective-permute-start.7 = (bf16[256,128]{1,0:T(8,128)(2,1)S(1)}, bf16[256,128]{1,0:T(8,128)(2,1)S(1)}, u32[]{:S(2)}, u32[]{:S(2)}) collective-permute-start(bf16[256,128]{1,0:T(8,128)(2,1)S(1)} %get-tuple-element.24), channel_id=1, source_target_pairs={{8,0},{16,8},{24,16},{32,24},{40,32},{48,40},{56,48},{64,56},{72,6... | collective-permute-start | bytes 196616 | tf_op jit(solution)/shard_map/ppermute | solution.py:28
  78.1 2.9 %collective-permute-start.13 = (bf16[256,128]{1,0:T(8,128)(2,1)S(1)}, bf16[256,128]{1,0:T(8,128)(2,1)S(1)}, u32[]{:S(2)}, u32[]{:S(2)}) collective-permute-start(bf16[256,128]{1,0:T(8,128)(2,1)S(1)} %get-tuple-element.36), channel_id=1, source_target_pairs={{16,0},{24,8},{32,16},{40,24},{48,32},{56,40},{64,48},{72,56},{80,... | collective-permute-start | bytes 196616 | tf_op jit(solution)/shard_map/ppermute | solution.py:28
  81.7 2.3 %collective-permute-done.13.r2 = bf16[256,128]{1,0:T(8,128)(2,1)S(1)} collective-permute-done((bf16[256,128]{1,0:T(8,128)(2,1)S(1)}, bf16[256,128]{1,0:T(8,128)(2,1)S(1)}, u32[]{:S(2)}, u32[]{:S(2)}) %collective-permute-start.13) | collective-permute-done | bytes 65568 | tf_op jit(solution)/shard_map/ppermute | solution.py:28
  84.1 2.8 %shard_map.114 = (bf16[4096,256]{1,0:T(8,128)(2,1)S(1)}, bf16[4096,128]{1,0:T(8,128)(2,1)}) custom-call(bf16[4096,256]{1,0:T(8,128)(2,1)S(1)} %copy-done, bf16[4096,128]{1,0:T(8,128)(2,1)S(1)} %bitcast.21, f32[256,128]{1,0:T(8,128)S(1)} %get-tuple-element.34.own, bf16[256,128]{1,0:T(8,128)(2,1)S(1)} %collective-permute-done.7.r1, ...), custom_call_target="tpu_custom_call" | custom-call | tf_op jit(solution)/shard_map/pallas_call | solution.py:256
  86.8 1.3 copy-done.1
  88.2 3.7 %all-to-all-start.2 = ((bf16[8,512,128]{2,1,0:T(8,128)(2,1)}), bf16[8,512,128]{2,1,0:T(8,128)(2,1)S(1)}, u32[]{:S(2)}, u32[]{:S(2)}) async-start(bf16[8,512,128]{2,1,0:T(8,128)(2,1)} %bitcast.11), calls=%async_computation.2 | async-start | bytes 2097152 | tf_op jit(solution)/shard_map/all_to_all | solution.py:32
  91.9 6.8 %shard_map.113 = (bf16[256,512]{1,0:T(8,128)(2,1)}, bf16[256,512]{1,0:T(8,128)(2,1)}, f32[256,128]{1,0:T(8,128)S(1)}, bf16[256,128]{1,0:T(8,128)(2,1)S(1)}, bf16...) custom-call(s32[1]{0:T(128)} %bitcast.base, bf16[256,512]{1,0:T(8,128)(2,1)S(1)} %bitcast.23, ...), custom_call_target="tpu_custom_call" | custom-call | tf_op jit(solution)/shard_map/pallas_call | solution.py:270
  98.6 1.6 %all-to-all-done.2.parts = bf16[8,512,128]{2,1,0:T(8,128)(2,1)S(1)} async-done(((bf16[8,512,128]{2,1,0:T(8,128)(2,1)}), bf16[8,512,128]{2,1,0:T(8,128)(2,1)S(1)}, u32[]{:S(2)}, u32[]{:S(2)}) %all-to-all-start.2) | async-done | bytes 1048608 | tf_op jit(solution)/shard_map/all_to_all | solution.py:32
  101.0 5.8 %all-to-all-start.3 = ((bf16[8,64,128]{2,1,0:T(8,128)(2,1)}), bf16[8,64,128]{2,1,0:T(8,128)(2,1)S(1)}, u32[]{:S(2)}, u32[]{:S(2)}) async-start(bf16[8,64,128]{2,1,0:T(8,128)(2,1)} %bitcast.12), calls=%async_computation.3 | async-start | bytes 262144 | tf_op jit(solution)/shard_map/all_to_all | solution.py:32
  106.9 7.1 %collective-permute-start.10 = (bf16[256,128]{1,0:T(8,128)(2,1)S(1)}, bf16[256,128]{1,0:T(8,128)(2,1)S(1)}, u32[]{:S(2)}, u32[]{:S(2)}) collective-permute-start(bf16[256,128]{1,0:T(8,128)(2,1)S(1)} %get-tuple-element.31), channel_id=1, source_target_pairs={{16,0},{24,8},{32,16},{40,24},{48,32},{56,40},{64,48},{72,56},{80,... | collective-permute-start | bytes 196616 | tf_op jit(solution)/shard_map/ppermute | solution.py:28
  114.0 4.0 %collective-permute-start.11 = (bf16[256,128]{1,0:T(8,128)(2,1)S(1)}, bf16[256,128]{1,0:T(8,128)(2,1)S(1)}, u32[]{:S(2)}, u32[]{:S(2)}) collective-permute-start(bf16[256,128]{1,0:T(8,128)(2,1)S(1)} %get-tuple-element.32), channel_id=1, source_target_pairs={{24,0},{32,8},{40,16},{48,24},{56,32},{64,40},{72,48},{80,56},{88,... | collective-permute-start | bytes 196616 | tf_op jit(solution)/shard_map/ppermute | solution.py:28
  118.0 4.3 %collective-permute-start.12 = (bf16[256,128]{1,0:T(8,128)(2,1)S(1)}, bf16[256,128]{1,0:T(8,128)(2,1)S(1)}, u32[]{:S(2)}, u32[]{:S(2)}) collective-permute-start(bf16[256,128]{1,0:T(8,128)(2,1)S(1)} %get-tuple-element.33), channel_id=1, source_target_pairs={{32,0},{40,8},{48,16},{56,24},{64,32},{72,40},{80,48},{88,56},{96,... | collective-permute-start | bytes 196616 | tf_op jit(solution)/shard_map/ppermute | solution.py:28
  122.2 3.1 %collective-permute-start.9 = (bf16[256,128]{1,0:T(8,128)(2,1)S(1)}, bf16[256,128]{1,0:T(8,128)(2,1)S(1)}, u32[]{:S(2)}, u32[]{:S(2)}) collective-permute-start(bf16[256,128]{1,0:T(8,128)(2,1)S(1)} %get-tuple-element.30), channel_id=1, source_target_pairs={{8,0},{16,8},{24,16},{32,24},{40,32},{48,40},{56,48},{64,56},{72,6... | collective-permute-start | bytes 196616 | tf_op jit(solution)/shard_map/ppermute | solution.py:28
  126.0 0.9 collective-permute-done.12.r4
  126.9 3.0 %collective-permute-done.9.r1 = bf16[256,128]{1,0:T(8,128)(2,1)S(1)} collective-permute-done((bf16[256,128]{1,0:T(8,128)(2,1)S(1)}, bf16[256,128]{1,0:T(8,128)(2,1)S(1)}, u32[]{:S(2)}, u32[]{:S(2)}) %collective-permute-start.9) | collective-permute-done | bytes 65568 | tf_op jit(solution)/shard_map/ppermute | solution.py:28
  131.3 9.1 %reduce-scatter.2.cloned.1.call-done = bf16[512,256]{1,0:T(8,128)(2,1)} async-done(((bf16[4096,256]{1,0:T(8,128)(2,1)}), bf16[512,256]{1,0:T(8,128)(2,1)}) %reduce-scatter.2.cloned.1.call-update) | async-done | bytes 262160 | tf_op jit(solution)/shard_map/reduce_scatter | solution.py:267
  (37 shorter events, 5.0 us)
Async XLA Ops:
  7.2 41.3 %copy-start = (bf16[4096,256]{1,0:T(8,128)(2,1)S(1)}, bf16[4096,256]{1,0:T(8,128)(2,1)}, u32[]{:S(2)}) copy-start(bf16[4096,256]{1,0:T(8,128)(2,1)} %x.1) | copy-start | bytes 6291460
  8.0 0.7 copy-start.8
  27.4 21.0 %all-to-all-start.1 = ((bf16[8,512,128]{2,1,0:T(8,128)(2,1)}), bf16[8,512,128]{2,1,0:T(8,128)(2,1)S(1)}, u32[]{:S(2)}, u32[]{:S(2)}) async-start(bf16[8,512,128]{2,1,0:T(8,128)(2,1)} %broadcast_in_dim.24), calls=%async_computation.1 | async-start | bytes 2097152 | tf_op jit(solution)/shard_map/all_to_all | solution.py:32
  32.6 21.7 %copy-start.2 = (bf16[256,1,512]{2,0,1:T(8,128)(2,1)S(1)}, bf16[256,1,512]{2,0,1:T(8,128)(2,1)}, u32[]{:S(2)}) copy-start(bf16[256,1,512]{2,0,1:T(8,128)(2,1)} %param.10) | copy-start | bytes 786436
  32.6 21.7 %copy-start.9 = (s32[256]{0:T(256)S(1)}, s32[256]{0:T(256)}, u32[]{:S(2)}) copy-start(s32[256]{0:T(256)} %param.12) | copy-start | bytes 3076
  32.6 107.8 %reduce-scatter.2.cloned.1.call-start = ((), (), s32[]{:S(2)}) async-start(), calls=%async_computation.5 | async-start | bytes 2359296 | tf_op jit(solution)/shard_map/reduce_scatter | solution.py:267
  32.7 18.6 %collective-permute-start = (bf16[256,128]{1,0:T(8,128)(2,1)}, bf16[256,128]{1,0:T(8,128)(2,1)}, u32[]{:S(2)}, u32[]{:S(2)}) collective-permute-start(bf16[256,128]{1,0:T(8,128)(2,1)} %bitcast.3.k0), channel_id=1, source_target_pairs={{0,8},{8,16},{16,24},{24,32},{32,40},{40,48},{48,56},{56,64},{64,7... | collective-permute-start | bytes 196616 | tf_op jit(solution)/shard_map/ppermute | solution.py:28
  35.2 18.5 %collective-permute-start.1 = (bf16[256,128]{1,0:T(8,128)(2,1)}, bf16[256,128]{1,0:T(8,128)(2,1)}, u32[]{:S(2)}, u32[]{:S(2)}) collective-permute-start(bf16[256,128]{1,0:T(8,128)(2,1)} %bitcast.3.k0), channel_id=1, source_target_pairs={{0,16},{8,24},{16,32},{24,40},{32,48},{40,56},{48,64},{56,72},{64,... | collective-permute-start | bytes 196616 | tf_op jit(solution)/shard_map/ppermute | solution.py:28
  37.2 16.5 %collective-permute-start.2 = (bf16[256,128]{1,0:T(8,128)(2,1)}, bf16[256,128]{1,0:T(8,128)(2,1)}, u32[]{:S(2)}, u32[]{:S(2)}) collective-permute-start(bf16[256,128]{1,0:T(8,128)(2,1)} %bitcast.3.k0), channel_id=1, source_target_pairs={{0,24},{8,32},{16,40},{24,48},{32,56},{40,64},{48,72},{56,80},{64,... | collective-permute-start | bytes 196616 | tf_op jit(solution)/shard_map/ppermute | solution.py:28
  42.0 12.4 %collective-permute-start.3 = (bf16[256,128]{1,0:T(8,128)(2,1)}, bf16[256,128]{1,0:T(8,128)(2,1)}, u32[]{:S(2)}, u32[]{:S(2)}) collective-permute-start(bf16[256,128]{1,0:T(8,128)(2,1)} %bitcast.3.k0), channel_id=1, source_target_pairs={{0,32},{8,40},{16,48},{24,56},{32,64},{40,72},{48,80},{56,88},{64,... | collective-permute-start | bytes 196616 | tf_op jit(solution)/shard_map/ppermute | solution.py:28
  49.4 17.5 %collective-permute-start.4 = (bf16[256,128]{1,0:T(8,128)(2,1)S(1)}, bf16[256,128]{1,0:T(8,128)(2,1)S(1)}, u32[]{:S(2)}, u32[]{:S(2)}) collective-permute-start(bf16[256,128]{1,0:T(8,128)(2,1)S(1)} %fusion.unused.v0), channel_id=1, source_target_pairs={{0,8},{8,16},{16,24},{24,32},{32,40},{40,48},{48,56},{56,64},{64,7... | collective-permute-start | bytes 196616 | tf_op jit(solution)/shard_map/ppermute | solution.py:28
  51.3 15.5 %collective-permute-start.5 = (bf16[256,128]{1,0:T(8,128)(2,1)S(1)}, bf16[256,128]{1,0:T(8,128)(2,1)}, u32[]{:S(2)}, u32[]{:S(2)}) collective-permute-start(bf16[256,128]{1,0:T(8,128)(2,1)S(1)} %fusion.unused.v0), channel_id=1, source_target_pairs={{0,16},{8,24},{16,32},{24,40},{32,48},{40,56},{48,64},{56,72},{64,... | collective-permute-start | bytes 196616 | tf_op jit(solution)/shard_map/ppermute | solution.py:28
  54.4 1.0 copy-start.3
  59.4 10.2 %collective-permute-start.6 = (bf16[512,128]{1,0:T(8,128)(2,1)S(1)}, bf16[512,128]{1,0:T(8,128)(2,1)S(1)}, u32[]{:S(2)}, u32[]{:S(2)}) collective-permute-start(bf16[512,128]{1,0:T(8,128)(2,1)S(1)} %get-tuple-element.23), channel_id=1, source_target_pairs={{16,0},{24,8},{32,16},{40,24},{48,32},{56,40},{64,48},{72,56},{80,... | collective-permute-start | bytes 393224 | tf_op jit(solution)/shard_map/ppermute | solution.py:28
  67.7 13.3 %collective-permute-start.8 = (bf16[512,128]{1,0:T(8,128)(2,1)S(1)}, bf16[512,128]{1,0:T(8,128)(2,1)S(1)}, u32[]{:S(2)}, u32[]{:S(2)}) collective-permute-start(bf16[512,128]{1,0:T(8,128)(2,1)S(1)} %pad_maximum_fusion), channel_id=1, source_target_pairs={{0,16},{8,24},{16,32},{24,40},{32,48},{40,56},{48,64},{56,72},{64,... | collective-permute-start | bytes 393224 | tf_op jit(solution)/shard_map/ppermute | solution.py:28
  69.7 11.3 %collective-permute-start.7 = (bf16[256,128]{1,0:T(8,128)(2,1)S(1)}, bf16[256,128]{1,0:T(8,128)(2,1)S(1)}, u32[]{:S(2)}, u32[]{:S(2)}) collective-permute-start(bf16[256,128]{1,0:T(8,128)(2,1)S(1)} %get-tuple-element.24), channel_id=1, source_target_pairs={{8,0},{16,8},{24,16},{32,24},{40,32},{48,40},{56,48},{64,56},{72,6... | collective-permute-start | bytes 196616 | tf_op jit(solution)/shard_map/ppermute | solution.py:28
  78.1 5.9 %collective-permute-start.13 = (bf16[256,128]{1,0:T(8,128)(2,1)S(1)}, bf16[256,128]{1,0:T(8,128)(2,1)S(1)}, u32[]{:S(2)}, u32[]{:S(2)}) collective-permute-start(bf16[256,128]{1,0:T(8,128)(2,1)S(1)} %get-tuple-element.36), channel_id=1, source_target_pairs={{16,0},{24,8},{32,16},{40,24},{48,32},{56,40},{64,48},{72,56},{80,... | collective-permute-start | bytes 196616 | tf_op jit(solution)/shard_map/ppermute | solution.py:28
  81.1 0.7 copy-start.5
  86.8 1.4 copy-start.1
  88.2 3.7 %copy-start.4 = (bf16[256,1,512]{2,0,1:T(8,128)(2,1)S(1)}, bf16[256,1,512]{2,0,1:T(8,128)(2,1)}, u32[]{:S(2)}) copy-start(bf16[256,1,512]{2,0,1:T(8,128)(2,1)} %param.13) | copy-start | bytes 786436
  88.2 3.7 %copy-start.6 = (bf16[512,128]{1,0:T(8,128)(2,1)S(1)}, bf16[512,128]{1,0:T(8,128)(2,1)}, u32[]{:S(2)}) copy-start(bf16[512,128]{1,0:T(8,128)(2,1)} %copy-done.5) | copy-start | bytes 393220
  88.2 12.1 %all-to-all-start.2 = ((bf16[8,512,128]{2,1,0:T(8,128)(2,1)}), bf16[8,512,128]{2,1,0:T(8,128)(2,1)S(1)}, u32[]{:S(2)}, u32[]{:S(2)}) async-start(bf16[8,512,128]{2,1,0:T(8,128)(2,1)} %bitcast.11), calls=%async_computation.2 | async-start | bytes 2097152 | tf_op jit(solution)/shard_map/all_to_all | solution.py:32
  101.0 24.3 %all-to-all-start.3 = ((bf16[8,64,128]{2,1,0:T(8,128)(2,1)}), bf16[8,64,128]{2,1,0:T(8,128)(2,1)S(1)}, u32[]{:S(2)}, u32[]{:S(2)}) async-start(bf16[8,64,128]{2,1,0:T(8,128)(2,1)} %bitcast.12), calls=%async_computation.3 | async-start | bytes 262144 | tf_op jit(solution)/shard_map/all_to_all | solution.py:32
  106.9 19.1 %collective-permute-start.10 = (bf16[256,128]{1,0:T(8,128)(2,1)S(1)}, bf16[256,128]{1,0:T(8,128)(2,1)S(1)}, u32[]{:S(2)}, u32[]{:S(2)}) collective-permute-start(bf16[256,128]{1,0:T(8,128)(2,1)S(1)} %get-tuple-element.31), channel_id=1, source_target_pairs={{16,0},{24,8},{32,16},{40,24},{48,32},{56,40},{64,48},{72,56},{80,... | collective-permute-start | bytes 196616 | tf_op jit(solution)/shard_map/ppermute | solution.py:28
  114.0 12.0 %collective-permute-start.11 = (bf16[256,128]{1,0:T(8,128)(2,1)S(1)}, bf16[256,128]{1,0:T(8,128)(2,1)S(1)}, u32[]{:S(2)}, u32[]{:S(2)}) collective-permute-start(bf16[256,128]{1,0:T(8,128)(2,1)S(1)} %get-tuple-element.32), channel_id=1, source_target_pairs={{24,0},{32,8},{40,16},{48,24},{56,32},{64,40},{72,48},{80,56},{88,... | collective-permute-start | bytes 196616 | tf_op jit(solution)/shard_map/ppermute | solution.py:28
  118.0 8.9 %collective-permute-start.12 = (bf16[256,128]{1,0:T(8,128)(2,1)S(1)}, bf16[256,128]{1,0:T(8,128)(2,1)S(1)}, u32[]{:S(2)}, u32[]{:S(2)}) collective-permute-start(bf16[256,128]{1,0:T(8,128)(2,1)S(1)} %get-tuple-element.33), channel_id=1, source_target_pairs={{32,0},{40,8},{48,16},{56,24},{64,32},{72,40},{80,48},{88,56},{96,... | collective-permute-start | bytes 196616 | tf_op jit(solution)/shard_map/ppermute | solution.py:28
  122.2 7.6 %collective-permute-start.9 = (bf16[256,128]{1,0:T(8,128)(2,1)S(1)}, bf16[256,128]{1,0:T(8,128)(2,1)S(1)}, u32[]{:S(2)}, u32[]{:S(2)}) collective-permute-start(bf16[256,128]{1,0:T(8,128)(2,1)S(1)} %get-tuple-element.30), channel_id=1, source_target_pairs={{8,0},{16,8},{24,16},{32,24},{40,32},{48,40},{56,48},{64,56},{72,6... | collective-permute-start | bytes 196616 | tf_op jit(solution)/shard_map/ppermute | solution.py:28
  129.9 0.8 copy-start.7
Sparse Core Ops, SparseCore 0:
  88.3 52.0 reduce-scatter.1
